TPU v7x, 32 devices: a whole 2x2x4 slice. The times are simulated.
32 devices in a mesh: task: 4 (over x, core), row: 8 (over z, y).
Axes of the slice: x: 2, y: 2, z: 4, core: 2. Of those that a mesh axis runs over, the one named last changes fastest.
Arguments:
- task_delta: bfloat16 [4, 28672, 4096], P('task', 'row'), may hold values from -16 to 16
- start_block: float32 [4, 4096, 32], P('task'), may hold values from -6 to 6
Outputs:
- merged: bfloat16 [28672, 4096], P(('row', 'task'))
All inputs are finite; a program needn't handle non-finite values.
Results may differ from a plain program's by a relative error of at most 0.013.
Values may be sent and summed in bfloat16 or wider, within the bound.
No kernel may reach another device: no remote copies, remote signals or barrier semaphores. Data moves between devices by JAX's collectives and lax.ppermute only.
A program may use at most 128 MiB of HBM per device.

v0:
```python
import jax
import jax.numpy as jnp
from jax import lax
from jax.sharding import PartitionSpec as P

ITERS = 4
ROOT_STEPS = 12


def matmul(left, right):
    return jnp.dot(left, right, precision=lax.Precision.HIGHEST, preferred_element_type=jnp.float32)


def inverse_root(gram):
    frob_norm = jnp.sqrt(jnp.sum(gram * gram))
    identity = jnp.eye(gram.shape[0], dtype=jnp.float32)
    upper = gram / frob_norm
    lower = identity
    for step in range(ROOT_STEPS):
        middle = 0.5 * (3.0 * identity - matmul(lower, upper))
        upper = matmul(upper, middle)
        lower = matmul(middle, lower)
    return lower / jnp.sqrt(frob_norm)


def orthonormal(backs, gram):
    factor = jnp.linalg.cholesky(gram)
    return lax.linalg.triangular_solve(factor, backs, left_side=False, lower=True, transpose_a=True)


def local(task_delta, start_block):
    local_rows = task_delta[0]
    current = start_block[0]
    for step in range(ITERS):
        narrow = current.astype(jnp.bfloat16)
        images = jnp.dot(local_rows, narrow, preferred_element_type=jnp.float32).astype(
            jnp.bfloat16
        )
        partial_value = lax.dot_general(
            local_rows, images, (((0,), (0,)), ((), ())), preferred_element_type=jnp.float32
        )
        backs = lax.psum(partial_value, "row")
        current = orthonormal(backs, matmul(backs.T, backs))
    projected = jnp.dot(
        local_rows, current.astype(jnp.bfloat16), preferred_element_type=jnp.float32
    ).astype(jnp.bfloat16)
    regrouped = lax.all_to_all(projected, "task", split_axis=0, concat_axis=1, tiled=True)
    bases = lax.all_gather(current, "task", axis=1, tiled=True)
    wide_proj = regrouped.astype(jnp.float32)
    left_gram = lax.psum(matmul(wide_proj.T, wide_proj), ("task", "row"))
    sing = jnp.sqrt(jnp.diagonal(left_gram))
    left_norm = left_gram / (sing[:, None] * sing[None, :])
    right_root = inverse_root(matmul(bases.T, bases))
    left_root = inverse_root(left_norm)
    mixing = left_root / sing[:, None] * sing[None, :]
    left_side = matmul(wide_proj, mixing)
    right_side = matmul(bases, right_root)
    return matmul(left_side, right_side.T).astype(jnp.bfloat16)


def solution(mesh):
    placed = (P("task", "row", None), P("task", None, None))
    return jax.shard_map(
        local, mesh=mesh, in_specs=placed, out_specs=P(("row", "task"), None), check_vma=False
    )
```

profile of v0, /device:TPU:0, one launch (start us, length us, event | category | flops | bytes accessed | tf_op | source)
XLA Modules:
  0.0 661.2 jit_solution(2960679549904435271)
XLA Ops:
  6.5 30.9 %fusion.18 = f32[4096,32]{0,1:T(8,128)} fusion(bf16[1,3584,4096]{2,1,0:T(8,128)(2,1)} %param.5, f32[1,4096,32]{1,2,0:T(8,128)} %param.6), kind=kOutput, calls=%fused_computation.20 | convolution fusion | flops 1879293952 | bytes 30408704 | tf_op jit(solution)/shard_map/dot_general | solution.py:39
  37.5 75.2 %all-reduce.6.cloned.1.call-done = f32[4096,32]{0,1:T(8,128)} async-done(((f32[4096,32]{0,1:T(8,128)}), f32[4096,32]{0,1:T(8,128)}) %all-reduce.6.cloned.1.call-update) | async-done | bytes 524304 | tf_op jit(solution)/shard_map/psum | solution.py:42
  112.7 1.8 fusion.113
  114.5 2.9 cholesky.74
  117.5 0.6 compare_reduce_fusion.3
  118.1 0.7 fusion.92
  118.8 2.4 custom-call.10
  121.2 1.7 fusion.30
  122.9 29.6 %fusion.21 = f32[4096,32]{0,1:T(8,128)} fusion(bf16[1,3584,4096]{2,1,0:T(8,128)(2,1)} %param.5, bf16[4096,32]{0,1:T(8,128)(2,1)S(1)} %fusion.30), kind=kOutput, calls=%fused_computation.21 | convolution fusion | flops 1879162880 | bytes 30146560 | tf_op jit(solution)/shard_map/dot_general | solution.py:39
  152.6 0.2 all-reduce.10.cloned.1.call-start
  152.8 71.6 %all-reduce.8.cloned.1.call-done = f32[4096,32]{0,1:T(8,128)} async-done(((f32[4096,32]{0,1:T(8,128)}), f32[4096,32]{0,1:T(8,128)}) %all-reduce.8.cloned.1.call-update) | async-done | bytes 524304 | tf_op jit(solution)/shard_map/psum | solution.py:42
  224.4 1.8 fusion.114
  226.2 2.9 cholesky.85
  229.1 0.6 compare_reduce_fusion.2
  229.8 0.7 fusion.93
  230.4 2.4 custom-call.11
  232.9 1.7 fusion.31
  234.6 29.6 %fusion.24 = f32[4096,32]{0,1:T(8,128)} fusion(bf16[1,3584,4096]{2,1,0:T(8,128)(2,1)} %param.5, bf16[4096,32]{0,1:T(8,128)(2,1)S(1)} %fusion.31), kind=kOutput, calls=%fused_computation.22 | convolution fusion | flops 1879162880 | bytes 30146560 | tf_op jit(solution)/shard_map/dot_general | solution.py:39
  264.3 71.7 %all-reduce.10.cloned.1.call-done = f32[4096,32]{0,1:T(8,128)} async-done(((f32[4096,32]{0,1:T(8,128)}), f32[4096,32]{0,1:T(8,128)}) %all-reduce.10.cloned.1.call-update) | async-done | bytes 524304 | tf_op jit(solution)/shard_map/psum | solution.py:42
  336.0 1.8 fusion.115
  337.9 2.9 cholesky.96
  340.8 0.6 compare_reduce_fusion.1
  341.5 0.7 fusion.94
  342.1 2.4 custom-call.12
  344.6 1.7 fusion.32
  346.3 29.6 %fusion.27 = f32[4096,32]{0,1:T(8,128)} fusion(bf16[1,3584,4096]{2,1,0:T(8,128)(2,1)} %param.5, bf16[4096,32]{0,1:T(8,128)(2,1)S(1)} %fusion.32), kind=kOutput, calls=%fused_computation.23 | convolution fusion | flops 1879162880 | bytes 30146560 | tf_op jit(solution)/shard_map/dot_general | solution.py:39
  375.9 71.8 %all-reduce.12.cloned.1.call-done = f32[4096,32]{0,1:T(8,128)} async-done(((f32[4096,32]{0,1:T(8,128)}), f32[4096,32]{0,1:T(8,128)}) %all-reduce.12.cloned.1.call-update) | async-done | bytes 524304 | tf_op jit(solution)/shard_map/psum | solution.py:42
  447.7 1.8 fusion.116
  449.6 2.9 cholesky.107
  452.5 0.6 compare_reduce_fusion
  453.2 0.7 fusion.95
  453.8 2.4 custom-call.13
  456.2 1.7 convolution_bitcast_fusion
  458.0 14.3 %fusion.53 = bf16[32,3584]{1,0:T(8,128)(2,1)S(1)} fusion(bf16[1,3584,4096]{2,1,0:T(8,128)(2,1)} %param.5, f32[4096,32]{0,1:T(8,128)S(1)} %convolution_bitcast_fusion), kind=kOutput, calls=%fused_computation.35 | convolution fusion | flops 939769856 | bytes 30113792 | tf_op jit(solution)/shard_map/dot_general | solution.py:44
  472.3 8.2 %all_to_all.19 = bf16[4,896,32]{1,2,0:T(8,128)(2,1)S(1)} all-to-all(bf16[4,896,32]{1,2,0:T(8,128)(2,1)S(1)} %bitcast.276), channel_id=1, replica_groups=mesh['task'=4,'row'=8] {'task'}, dimensions={0} | all-to-all | bytes 458752 | tf_op jit(solution)/shard_map/all_to_all | solution.py:47
  480.6 0.8 fusion.117
  481.4 0.3 all-gather.2.cloned.1.call-start
  481.7 0.3 all-gather.2.cloned.1.call-update
  482.0 115.5 %all-reduce.14.cloned.1.call-done = f32[128,128]{1,0:T(8,128)} async-done(((f32[128,128]{1,0:T(8,128)}), f32[128,128]{1,0:T(8,128)}) %all-reduce.14.cloned.1.call-update) | async-done | bytes 65552 | tf_op jit(solution)/shard_map/psum | solution.py:50
  597.5 1.9 gather_fusion
  599.5 1.6 fusion.90
  601.8 1.1 fusion.80
  603.1 1.1 fusion.110
  604.2 0.2 fusion.79
  604.4 0.2 fusion.119
  604.8 0.2 fusion.78
  605.5 0.2 fusion.77
  606.7 0.2 fusion.75
  607.4 0.2 fusion.74
  608.0 0.2 fusion.73
  608.7 0.2 fusion.72
  609.3 0.2 fusion.71
  609.9 0.2 fusion.70
  610.6 0.2 fusion.69
  610.8 0.2 fusion.68
  611.0 0.4 fusion.138
  611.4 11.2 %all-gather.2.cloned.1.call-done = f32[4096,128]{0,1:T(8,128)} async-done(((f32[4096,32]{0,1:T(8,128)}), f32[4096,128]{0,1:T(8,128)}) %all-gather.2.cloned.1.call-update) | async-done | bytes 2097168 | tf_op jit(solution)/shard_map/all_gather | solution.py:48
  622.5 4.7 multiply_reduce_fusion
  628.5 0.2 fusion.66
  630.4 0.2 fusion.63
  632.3 0.2 fusion.60
  633.6 0.2 fusion.58
  635.3 5.3 fusion.159
  640.6 13.4 %convolution_convert_fusion = bf16[896,4096]{1,0:T(8,128)(2,1)} fusion(f32[896,128]{1,0:T(8,128)S(1)} %fusion.138, f32[4096,128]{1,0:T(8,128)S(1)} %fusion.159), kind=kOutput, calls=%fused_computation.19 | convolution fusion | flops 5640814592 | bytes 9895936 | tf_op jit(solution)/shard_map/dot_general | solution.py:11
  (79 shorter events, 11.2 us)
Async XLA Ops:
  6.5 106.1 %all-reduce.6.cloned.1.call-start = ((), (), s32[]{:S(2)}) async-start(), calls=%async_computation.1 | async-start | bytes 1048576 | tf_op jit(solution)/shard_map/psum | solution.py:42
  37.4 186.9 %all-reduce.8.cloned.1.call-start = ((), (), s32[]{:S(2)}) async-start(), calls=%async_computation.2 | async-start | bytes 1048576 | tf_op jit(solution)/shard_map/psum | solution.py:42
  152.6 183.5 %all-reduce.10.cloned.1.call-start = ((), (), s32[]{:S(2)}) async-start(), calls=%async_computation.3 | async-start | bytes 1048576 | tf_op jit(solution)/shard_map/psum | solution.py:42
  264.2 183.5 %all-reduce.12.cloned.1.call-start = ((), (), s32[]{:S(2)}) async-start(), calls=%async_computation.4 | async-start | bytes 1048576 | tf_op jit(solution)/shard_map/psum | solution.py:42
  375.9 221.6 %all-reduce.14.cloned.1.call-start = ((), (), s32[]{:S(2)}) async-start(), calls=%async_computation.5 | async-start | bytes 131072 | tf_op jit(solution)/shard_map/psum | solution.py:50
  457.9 23.8 %copy-start = (f32[4096,32]{0,1:T(8,128)}, f32[4096,32]{0,1:T(8,128)S(1)}, u32[]{:S(2)}) copy-start(f32[4096,32]{0,1:T(8,128)S(1)} %convolution_bitcast_fusion) | copy-start | bytes 1572868
  481.4 141.1 %all-gather.2.cloned.1.call-start = ((), (), s32[]{:S(2)}) async-start(), calls=%async_computation.6 | async-start | bytes 2621440 | tf_op jit(solution)/shard_map/all_gather | solution.py:48
Sparse Core Ops, SparseCore 0:
  37.5 75.0 all-reduce.5
  152.7 71.6 all-reduce.7
  264.3 71.6 all-reduce.9
  376.0 71.6 all-reduce.11
  481.6 115.9 all-reduce.13
  598.9 23.5 all-gather.1
where the time goes:
time: 668 us; the launch traced here: 661 us
  waiting for transfers between devices  417 us (62%)
  matrix products  188 us (28%)
  other arithmetic  28.4 us (4%)
  between operations  16.1 us (2%)
  blocking collectives  8.22 us (1%)
    psum x4, waiting for transfers between devices, local(): backs = lax.psum(partial_value, 'row')  290 us
    dot_general x4, matrix products, local(): lax.dot_general(local_rows, images, (((0,), (0,)), ((), ())), preferred_e...  120 us
    psum x1, waiting for transfers between devices, local(): left_gram = lax.psum(matmul(wide_proj.T, wide_proj), ('task', 'row'))  116 us
    dot_general x79, matrix products, matmul(): jnp.dot(left, right, precision=lax.Precision.HIGHEST, preferred_element_t...  47.6 us
    another operation x12, other arithmetic, orthonormal(): factor = jnp.linalg.cholesky(gram)  14.4 us
    dot_general x1, matrix products, local(): jnp.dot(local_rows, current.astype(jnp.bfloat16), preferred_element_type=...  14.3 us
  transfers between devices with their start and end apart: 6, of which 6 were waited for; matrix products, arithmetic and copies ran while one was open for 2% of the time, Pallas kernels for 0%

commit v1 on v0

v1 whole, which is shorter than its diff:
```python
import functools

import jax
import jax.numpy as jnp
from jax import lax
from jax.experimental import pallas as pl
from jax.experimental.pallas import tpu as pltpu
from jax.sharding import PartitionSpec as P

ITERS = 4
ROOT_STEPS = 12
LANES = 128
F32 = jnp.float32
BF16 = jnp.bfloat16
ROWS_BY_ROWS = (((1,), (1,)), ((), ()))
VMEM_BYTES = 56 * 1024 * 1024


def params():
    return pltpu.CompilerParams(vmem_limit_bytes=VMEM_BYTES)


def exact(left, right, dims=(((1,), (0,)), ((), ()))):
    return lax.dot_general(left, right, dims, precision=lax.Precision.HIGHEST, preferred_element_type=F32)


def split_two(value):
    high = value.astype(BF16)
    return high, (value - high.astype(F32)).astype(BF16)


def split_three(value):
    high = value.astype(BF16)
    rest = value - high.astype(F32)
    middle = rest.astype(BF16)
    return high, middle, (rest - middle.astype(F32)).astype(BF16)


def spread(value, order, axis):
    pieces = split_three(value)
    return jnp.concatenate([pieces[at] for at in order], axis=axis)


def square(left, right):
    return jnp.dot(
        spread(left, (0, 0, 1, 0, 2, 1), 1), spread(right, (0, 1, 0, 2, 0, 1), 0), preferred_element_type=F32
    )


def lower_inverse(gram):
    count, size, _ = gram.shape
    rows = lax.broadcasted_iota(jnp.int32, (size, 1), 0)
    eye = (
        lax.broadcasted_iota(jnp.int32, (size, size), 0) == lax.broadcasted_iota(jnp.int32, (size, size), 1)
    ).astype(F32)
    work = [jnp.concatenate([gram[at], eye], axis=1) for at in range(count)]
    scale = [jnp.zeros((size, 1), F32) for _ in range(count)]
    for step in range(size):
        for at in range(count):
            pivot = work[at][step : step + 1, step : step + 1]
            row = work[at][step : step + 1, :] / pivot
            col = jnp.where(rows > step, work[at][:, step : step + 1], 0.0)
            scale[at] = jnp.where(rows == step, lax.rsqrt(pivot), scale[at])
            work[at] = work[at] - col * row
    return [work[at][:, size:] * scale[at] for at in range(count)]


def sweep_kernel(parts, x_ref, d_ref, out_ref, wide, total, gram):
    step = pl.program_id(0)
    rank = x_ref.shape[1]
    chunk = x_ref.shape[2]

    @pl.when(step == 0)
    def _():
        for part in range(parts):
            wide[:, part * chunk : (part + 1) * chunk] = x_ref[part]
        total[...] = jnp.zeros_like(total)
        gram[...] = jnp.zeros_like(gram)

    images = lax.dot_general(d_ref[...], wide[...], ROWS_BY_ROWS, preferred_element_type=F32)
    flipped = images.T.astype(BF16)
    total[...] += jnp.dot(flipped, d_ref[...], preferred_element_type=F32)
    gram[...] += lax.dot_general(flipped, flipped, ROWS_BY_ROWS, preferred_element_type=F32)

    @pl.when(step == pl.num_programs(0) - 1)
    def _():
        spare = jnp.zeros((rank, LANES - 3 * rank), BF16)
        pieces = jnp.concatenate([*split_three(gram[...]), spare], axis=1)
        for part in range(parts):
            out_ref[part, :, :chunk] = total[:, part * chunk : (part + 1) * chunk].astype(BF16)
            out_ref[part, :, chunk:] = pieces


def sweep(delta, block):
    rows, cols = delta.shape
    parts, rank, chunk = block.shape
    tall = next(size for size in (512, 448, rows) if rows % size == 0)
    return pl.pallas_call(
        functools.partial(sweep_kernel, parts),
        out_shape=jax.ShapeDtypeStruct((parts, rank, chunk + LANES), BF16),
        grid=(rows // tall,),
        in_specs=[
            pl.BlockSpec((parts, rank, chunk), lambda at: (0, 0, 0)),
            pl.BlockSpec((tall, cols), lambda at: (at, 0)),
        ],
        out_specs=pl.BlockSpec((parts, rank, chunk + LANES), lambda at: (0, 0, 0)),
        scratch_shapes=[
            pltpu.VMEM((rank, cols), BF16),
            pltpu.VMEM((rank, cols), F32),
            pltpu.VMEM((rank, rank), F32),
        ],
        cost_estimate=pl.CostEstimate(flops=4 * rows * cols * rank, bytes_accessed=2 * rows * cols, transcendentals=0),
        compiler_params=params(),
        name="sweep",
    )(block, delta)


def settle_kernel(in_ref, out_ref):
    parts, rank, wide = in_ref.shape
    chunk = wide - LANES
    total = in_ref[0].astype(F32)
    for part in range(1, parts):
        total = total + in_ref[part].astype(F32)
    tail = total[:, chunk:]
    gram = tail[:, :rank] + tail[:, rank : 2 * rank] + tail[:, 2 * rank : 3 * rank]
    out_ref[...] = exact(lower_inverse(gram[None])[0], total[:, :chunk]).astype(BF16)


def settle(pieces):
    parts, rank, wide = pieces.shape
    return pl.pallas_call(
        settle_kernel,
        out_shape=jax.ShapeDtypeStruct((rank, wide - LANES), BF16),
        compiler_params=params(),
        name="settle",
    )(pieces)


def project_kernel(parts, x_ref, d_ref, out_ref, wide):
    chunk = x_ref.shape[2]

    @pl.when(pl.program_id(0) == 0)
    def _():
        for part in range(parts):
            wide[:, part * chunk : (part + 1) * chunk] = x_ref[part]

    images = lax.dot_general(d_ref[...], wide[...], ROWS_BY_ROWS, preferred_element_type=F32)
    out_ref[0] = images.T.astype(BF16)


def project(delta, block, tasks):
    rows, cols = delta.shape
    parts, rank, chunk = block.shape
    tall = rows // tasks
    return pl.pallas_call(
        functools.partial(project_kernel, parts),
        out_shape=jax.ShapeDtypeStruct((tasks, rank, tall), BF16),
        grid=(tasks,),
        in_specs=[
            pl.BlockSpec((parts, rank, chunk), lambda at: (0, 0, 0)),
            pl.BlockSpec((tall, cols), lambda at: (at, 0)),
        ],
        out_specs=pl.BlockSpec((1, rank, tall), lambda at: (at, 0, 0)),
        scratch_shapes=[pltpu.VMEM((rank, cols), BF16)],
        cost_estimate=pl.CostEstimate(flops=2 * rows * cols * rank, bytes_accessed=2 * rows * cols, transcendentals=0),
        compiler_params=params(),
        name="project",
    )(block, delta)


def gram_kernel(in_ref, out_ref):
    flat = in_ref[...].reshape(-1, in_ref.shape[2])
    out_ref[...] = lax.dot_general(flat, flat, ROWS_BY_ROWS, preferred_element_type=F32).reshape(out_ref.shape)


def left_partial(images, parts):
    tasks, rank, _ = images.shape
    size = tasks * rank
    return pl.pallas_call(
        gram_kernel,
        out_shape=jax.ShapeDtypeStruct((parts, size // parts, size), F32),
        compiler_params=params(),
        name="left_partial",
    )(images)


def roots_of(grams):
    size = grams[0].shape[0]
    identity = (
        lax.broadcasted_iota(jnp.int32, (size, size), 0) == lax.broadcasted_iota(jnp.int32, (size, size), 1)
    ).astype(F32)
    norms = [jnp.sqrt(jnp.sum(gram * gram)) for gram in grams]
    state = tuple((gram / norm, identity) for gram, norm in zip(grams, norms))

    def step(_, state):
        out = []
        for upper, lower in state:
            middle = 0.5 * (3.0 * identity - square(lower, upper))
            out.append((square(upper, middle), square(middle, lower)))
        return tuple(out)

    state = lax.fori_loop(0, ROOT_STEPS, step, state)
    return [lower / jnp.sqrt(norm) for (_, lower), norm in zip(state, norms)]


def mix_kernel(tasks, left_ref, y_ref, out_ref, lower):
    parts, rows, size = left_ref.shape[1:]
    rank = size // tasks
    left_raw = left_ref[0]
    for task in range(1, tasks):
        left_raw = left_raw + left_ref[task]
    left_raw = left_raw.reshape(size, size)
    right_raw = jnp.zeros((size, size), F32)
    for part in range(y_ref.shape[1]):
        piece = y_ref[:, part].reshape(size, y_ref.shape[3])
        right_raw = right_raw + lax.dot_general(piece, piece, ROWS_BY_ROWS, preferred_element_type=F32)
    blocks = jnp.stack(
        [
            right_raw[task * rank : (task + 1) * rank, task * rank : (task + 1) * rank]
            for task in range(tasks)
        ]
    )
    lower[...] = jnp.zeros_like(lower)
    for task, inverse in enumerate(lower_inverse(blocks)):
        lower[task * rank : (task + 1) * rank, task * rank : (task + 1) * rank] = inverse
    change = lower[...]
    right_gram = square(square(change, right_raw), change.T)
    left_gram = square(square(change, left_raw), change.T)
    diagonal = lax.broadcasted_iota(jnp.int32, (size, size), 0) == lax.broadcasted_iota(jnp.int32, (size, size), 1)
    on_diagonal = jnp.where(diagonal, left_gram, 0.0)
    sing_down = jnp.sqrt(jnp.sum(on_diagonal, axis=1, keepdims=True))
    sing_across = jnp.sqrt(jnp.sum(on_diagonal, axis=0, keepdims=True))
    left_root, right_root = roots_of([left_gram / (sing_down * sing_across), right_gram])
    mixing = left_root / sing_down * sing_across
    inner = square(mixing, right_root.T)
    out_ref[...] = square(square(change.T, inner), change)


def mix(left_pieces, bases):
    tasks, parts, rows, size = left_pieces.shape
    return pl.pallas_call(
        functools.partial(mix_kernel, tasks),
        out_shape=jax.ShapeDtypeStruct((size, size), F32),
        scratch_shapes=[pltpu.VMEM((size, size), F32)],
        compiler_params=params(),
        name="mix",
    )(left_pieces, bases)


def merge_kernel(mix_ref, p_ref, y_ref, out_ref, left):
    size = mix_ref.shape[0]

    @pl.when(pl.program_id(0) == 0)
    def _():
        images = p_ref[...].reshape(size, p_ref.shape[2]).T
        high, low = split_two(mix_ref[...])
        side = jnp.dot(images, high, preferred_element_type=F32) + jnp.dot(images, low, preferred_element_type=F32)
        left[...] = jnp.concatenate(split_two(side), axis=1)

    bases = y_ref[...].reshape(size, y_ref.shape[3])
    bases = jnp.concatenate([bases, bases], axis=0)
    out_ref[...] = jnp.dot(left[...], bases, preferred_element_type=F32).astype(BF16)


def merge(mixed, images, bases):
    tasks, parts, rank, chunk = bases.shape
    rows = images.shape[2]
    size = tasks * rank
    return pl.pallas_call(
        merge_kernel,
        out_shape=jax.ShapeDtypeStruct((rows, parts * chunk), BF16),
        grid=(parts,),
        in_specs=[
            pl.BlockSpec((size, size), lambda at: (0, 0)),
            pl.BlockSpec((tasks, rank, rows), lambda at: (0, 0, 0)),
            pl.BlockSpec((tasks, 1, rank, chunk), lambda at: (0, at, 0, 0)),
        ],
        out_specs=pl.BlockSpec((rows, chunk), lambda at: (0, at)),
        scratch_shapes=[pltpu.VMEM((rows, 2 * size), BF16)],
        compiler_params=params(),
        name="merge",
    )(mixed, images, bases)


def swap(pieces, axis):
    return lax.all_to_all(pieces, axis, split_axis=0, concat_axis=0, tiled=True)


def share(piece, axis, count):
    return swap(jnp.broadcast_to(piece[None], (count, *piece.shape)), axis)


def local(tasks, parts, task_delta, start_block):
    delta = task_delta[0]
    cols, rank = start_block.shape[1:]
    block = start_block[0].T.astype(BF16).reshape(rank, parts, cols // parts).transpose(1, 0, 2)
    for step in range(ITERS):
        block = share(settle(swap(sweep(delta, block), "row")), "row", parts)
    gathered = [block]
    for shift in range(1, tasks):
        gathered.append(lax.ppermute(block, "task", [(at, (at + shift) % tasks) for at in range(tasks)]))
    images = swap(project(delta, block, tasks), "task")
    own = lax.axis_index("task")
    bases = jnp.stack(gathered)[(own - jnp.arange(tasks)) % tasks]
    partial = jnp.sum(swap(left_partial(images, parts), "row"), axis=0)
    left_pieces = share(partial, ("task", "row"), tasks * parts).reshape(tasks, parts, *partial.shape)
    return merge(mix(left_pieces, bases), images, bases)


def solution(mesh):
    tasks, parts = mesh.shape["task"], mesh.shape["row"]
    placed = (P("task", "row", None), P("task", None, None))
    return jax.shard_map(
        functools.partial(local, tasks, parts),
        mesh=mesh,
        in_specs=placed,
        out_specs=P(("row", "task"), None),
        check_vma=False,
    )
```

time: 668 us -> 312 us (0.47)
  waiting for transfers between devices: 417 us -> 14.9 us
  matrix products: 188 us -> 0 us
  Pallas kernels: 0 us -> 156 us
  blocking collectives: 8.22 us -> 126 us
  other arithmetic: 28.4 us -> 1.23 us
  between operations: 16.1 us -> 0.07 us
    psum x5 -> x0, waiting for transfers between devices: 406 us -> none  [the longest x4 290 us: local(): backs = lax.psum(partial_value, 'row')]
    dot_general x84 -> x0, matrix products: 182 us -> none  [the longest x4 120 us: local(): lax.dot_general(local_rows, images, (((0,), (0,)), ((), ())), preferred_e...]
    pallas_call x0 -> x12, Pallas kernels: none -> 156 us  [the longest x4 95.4 us: sweep(): pl.pallas_call(functools.partial(sweep_kernel, parts), out_shape=jax.Shap...]
    all_to_all x1 -> x10, blocking collectives: 8.22 us -> 126 us  [swap(): return lax.all_to_all(pieces, axis, split_axis=0, concat_axis=0, tiled=True)]
    another operation x21 -> x1, other arithmetic: 26.7 us -> 0.13 us  [local(): bases = jnp.stack(gathered)[(own - jnp.arange(tasks)) % tasks]]
    ppermute x0 -> x3, waiting for transfers between devices: none -> 14.9 us  [local(): lax.ppermute(block, 'task', [(at, (at + shift) % tasks) for at in range(t...]
    all_gather x1 -> x0, waiting for transfers between devices: 11.2 us -> none  [local(): bases = lax.all_gather(current, 'task', axis=1, tiled=True)]
    another operation x4 -> x0, matrix products: 6.76 us -> none  [orthonormal(): lax.linalg.triangular_solve(factor, backs, left_side=False, lower=True, t...]
  transfers between devices with their start and end apart: 6 -> 4, of which waited for: 6 -> 2; matrix products, arithmetic and copies ran while one was open for 2% -> 1% of each run, Pallas kernels for 0% -> 0%
where the time goes in v1:
time: 312 us; the launch traced here: 310 us
  Pallas kernels  156 us (50%)
  blocking collectives  126 us (40%)
  waiting for transfers between devices  14.9 us (5%)
  local copies, waits for them, and re-layouts  6.82 us (2%)
  starting transfers between devices  4.53 us (1%)
    all_to_all x10, blocking collectives, swap(): return lax.all_to_all(pieces, axis, split_axis=0, concat_axis=0, tiled=True)  126 us
    pallas_call x4, Pallas kernels, sweep(): pl.pallas_call(functools.partial(sweep_kernel, parts), out_shape=jax.Shap...  95.4 us
    pallas_call x4, Pallas kernels, settle(): pl.pallas_call(settle_kernel, out_shape=jax.ShapeDtypeStruct((rank, wide...  18.8 us
    pallas_call x1, Pallas kernels, mix(): pl.pallas_call(functools.partial(mix_kernel, tasks), out_shape=jax.ShapeD...  17 us
    pallas_call x1, Pallas kernels, project(): pl.pallas_call(functools.partial(project_kernel, parts), out_shape=jax.Sh...  15.4 us
    ppermute x3, waiting for transfers between devices, local(): lax.ppermute(block, 'task', [(at, (at + shift) % tasks) for at in range(t...  14.9 us
    pallas_call x1, Pallas kernels, merge(): pl.pallas_call(merge_kernel, out_shape=jax.ShapeDtypeStruct((rows, parts...  8.07 us
  transfers between devices with their start and end apart: 4, of which 2 were waited for; matrix products, arithmetic and copies ran while one was open for 1% of the time, Pallas kernels for 0%

profile of v1, /device:TPU:0, one launch (start us, length us, event | category | flops | bytes accessed | tf_op | source)
XLA Modules:
  0.0 309.9 jit_solution(2312064883916655132)
XLA Ops:
  0.0 1.1 convert_element_type.9
  1.1 0.7 copy.6
  1.8 23.9 %sweep.4 = bf16[8,32,640]{2,1,0:T(8,128)(2,1)} custom-call(bf16[8,32,512]{2,1,0:T(8,128)(2,1)} %bitcast.24, bf16[3584,4096]{1,0:T(8,128)(2,1)} %bitcast.18), custom_call_target="tpu_custom_call" | custom-call | flops 1879048192 | bytes 29360128 | tf_op jit(solution)/shard_map/sweep/pallas_call | solution.py:98
  25.6 18.3 %all_to_all.55.in_ref = bf16[8,32,640]{2,1,0:T(8,128)(2,1)} all-to-all(bf16[8,32,640]{2,1,0:T(8,128)(2,1)} %sweep.4), channel_id=1, replica_groups=mesh['task'=4,'row'=8] {'row'}, dimensions={0} | all-to-all | bytes 655360 | tf_op jit(solution)/shard_map/all_to_all | solution.py:286
  43.9 4.7 %settle.4 = bf16[32,512]{1,0:T(8,128)(2,1)} custom-call(bf16[8,32,640]{2,1,0:T(8,128)(2,1)} %all_to_all.55.in_ref), custom_call_target="tpu_custom_call" | custom-call | tf_op jit(solution)/shard_map/settle/pallas_call | solution.py:131
  48.6 0.8 broadcast_in_dim.10
  49.4 11.6 %all_to_all.56.x_ref = bf16[8,32,512]{2,1,0:T(8,128)(2,1)} all-to-all(bf16[8,32,512]{2,1,0:T(8,128)(2,1)S(1)} %broadcast_in_dim.10), channel_id=1, replica_groups=mesh['task'=4,'row'=8] {'row'}, dimensions={0} | all-to-all | bytes 524288 | tf_op jit(solution)/shard_map/all_to_all | solution.py:286
  61.1 23.9 %sweep.5 = bf16[8,32,640]{2,1,0:T(8,128)(2,1)} custom-call(bf16[8,32,512]{2,1,0:T(8,128)(2,1)} %all_to_all.56.x_ref, bf16[3584,4096]{1,0:T(8,128)(2,1)} %bitcast.19), custom_call_target="tpu_custom_call" | custom-call | flops 1879048192 | bytes 29360128 | tf_op jit(solution)/shard_map/sweep/pallas_call | solution.py:98
  84.9 14.1 %all_to_all.57.in_ref = bf16[8,32,640]{2,1,0:T(8,128)(2,1)} all-to-all(bf16[8,32,640]{2,1,0:T(8,128)(2,1)} %sweep.5), channel_id=1, replica_groups=mesh['task'=4,'row'=8] {'row'}, dimensions={0} | all-to-all | bytes 655360 | tf_op jit(solution)/shard_map/all_to_all | solution.py:286
  99.0 4.7 %settle.5 = bf16[32,512]{1,0:T(8,128)(2,1)} custom-call(bf16[8,32,640]{2,1,0:T(8,128)(2,1)} %all_to_all.57.in_ref), custom_call_target="tpu_custom_call" | custom-call | tf_op jit(solution)/shard_map/settle/pallas_call | solution.py:131
  103.7 0.8 broadcast_in_dim.11
  104.5 11.5 %all_to_all.58.x_ref = bf16[8,32,512]{2,1,0:T(8,128)(2,1)} all-to-all(bf16[8,32,512]{2,1,0:T(8,128)(2,1)S(1)} %broadcast_in_dim.11), channel_id=1, replica_groups=mesh['task'=4,'row'=8] {'row'}, dimensions={0} | all-to-all | bytes 524288 | tf_op jit(solution)/shard_map/all_to_all | solution.py:286
  116.0 23.9 %sweep.6 = bf16[8,32,640]{2,1,0:T(8,128)(2,1)} custom-call(bf16[8,32,512]{2,1,0:T(8,128)(2,1)} %all_to_all.58.x_ref, bf16[3584,4096]{1,0:T(8,128)(2,1)} %bitcast.20), custom_call_target="tpu_custom_call" | custom-call | flops 1879048192 | bytes 29360128 | tf_op jit(solution)/shard_map/sweep/pallas_call | solution.py:98
  139.8 14.0 %all_to_all.59.in_ref = bf16[8,32,640]{2,1,0:T(8,128)(2,1)} all-to-all(bf16[8,32,640]{2,1,0:T(8,128)(2,1)} %sweep.6), channel_id=1, replica_groups=mesh['task'=4,'row'=8] {'row'}, dimensions={0} | all-to-all | bytes 655360 | tf_op jit(solution)/shard_map/all_to_all | solution.py:286
  153.8 4.7 %settle.6 = bf16[32,512]{1,0:T(8,128)(2,1)} custom-call(bf16[8,32,640]{2,1,0:T(8,128)(2,1)} %all_to_all.59.in_ref), custom_call_target="tpu_custom_call" | custom-call | tf_op jit(solution)/shard_map/settle/pallas_call | solution.py:131
  158.5 0.8 broadcast_in_dim.12
  159.3 11.3 %all_to_all.60.x_ref = bf16[8,32,512]{2,1,0:T(8,128)(2,1)} all-to-all(bf16[8,32,512]{2,1,0:T(8,128)(2,1)S(1)} %broadcast_in_dim.12), channel_id=1, replica_groups=mesh['task'=4,'row'=8] {'row'}, dimensions={0} | all-to-all | bytes 524288 | tf_op jit(solution)/shard_map/all_to_all | solution.py:286
  170.6 23.9 %sweep.7 = bf16[8,32,640]{2,1,0:T(8,128)(2,1)} custom-call(bf16[8,32,512]{2,1,0:T(8,128)(2,1)} %all_to_all.60.x_ref, bf16[3584,4096]{1,0:T(8,128)(2,1)} %bitcast.21), custom_call_target="tpu_custom_call" | custom-call | flops 1879048192 | bytes 29360128 | tf_op jit(solution)/shard_map/sweep/pallas_call | solution.py:98
  194.4 13.8 %all_to_all.61.in_ref = bf16[8,32,640]{2,1,0:T(8,128)(2,1)} all-to-all(bf16[8,32,640]{2,1,0:T(8,128)(2,1)} %sweep.7), channel_id=1, replica_groups=mesh['task'=4,'row'=8] {'row'}, dimensions={0} | all-to-all | bytes 655360 | tf_op jit(solution)/shard_map/all_to_all | solution.py:286
  208.2 4.7 %settle.7 = bf16[32,512]{1,0:T(8,128)(2,1)} custom-call(bf16[8,32,640]{2,1,0:T(8,128)(2,1)} %all_to_all.61.in_ref), custom_call_target="tpu_custom_call" | custom-call | tf_op jit(solution)/shard_map/settle/pallas_call | solution.py:131
  212.9 0.8 broadcast_in_dim.13
  213.7 11.3 %all_to_all.62.x_ref = bf16[8,32,512]{2,1,0:T(8,128)(2,1)} all-to-all(bf16[8,32,512]{2,1,0:T(8,128)(2,1)S(1)} %broadcast_in_dim.13), channel_id=1, replica_groups=mesh['task'=4,'row'=8] {'row'}, dimensions={0} | all-to-all | bytes 524288 | tf_op jit(solution)/shard_map/all_to_all | solution.py:286
  225.0 0.0 copy-start
  225.0 15.4 %project.1 = bf16[4,32,896]{2,1,0:T(8,128)(2,1)} custom-call(bf16[8,32,512]{2,1,0:T(8,128)(2,1)} %all_to_all.62.x_ref, bf16[3584,4096]{1,0:T(8,128)(2,1)} %bitcast.22), custom_call_target="tpu_custom_call" | custom-call | flops 939524096 | bytes 29360128 | tf_op jit(solution)/shard_map/project/pallas_call | solution.py:155
  240.3 9.8 %all_to_all.63.in_ref.p_ref = bf16[4,32,896]{2,1,0:T(8,128)(2,1)} all-to-all(bf16[4,32,896]{2,1,0:T(8,128)(2,1)} %project.1), channel_id=1, replica_groups=mesh['task'=4,'row'=8] {'task'}, dimensions={0} | all-to-all | bytes 458752 | tf_op jit(solution)/shard_map/all_to_all | solution.py:286
  250.1 1.8 left_partial.1
  251.9 10.3 %all_to_all.64 = f32[8,16,128]{2,1,0:T(8,128)S(1)} all-to-all(f32[8,16,128]{2,1,0:T(8,128)} %left_partial.1), channel_id=1, replica_groups=mesh['task'=4,'row'=8] {'row'}, dimensions={0} | all-to-all | bytes 131072 | tf_op jit(solution)/shard_map/all_to_all | solution.py:286
  262.2 0.7 broadcast_in_dim.14
  262.9 2.6 all-to-all-start.10
  265.5 0.0 copy-done
  265.6 1.4 collective-permute-start.2
  267.0 0.4 collective-permute-start.1
  267.3 0.1 collective-permute-start
  267.5 7.9 %collective-permute-done.2 = bf16[8,32,512]{2,1,0:T(8,128)(2,1)S(1)} collective-permute-done((bf16[8,32,512]{2,1,0:T(8,128)(2,1)S(1)}, bf16[8,32,512]{2,1,0:T(8,128)(2,1)S(1)}, u32[]{:S(2)}, u32[]{:S(2)}) %collective-permute-start.2) | collective-permute-done | bytes 262176 | tf_op jit(solution)/shard_map/ppermute | solution.py:301
  275.4 7.0 %collective-permute-done.1 = bf16[8,32,512]{2,1,0:T(8,128)(2,1)S(1)} collective-permute-done((bf16[8,32,512]{2,1,0:T(8,128)(2,1)S(1)}, bf16[8,32,512]{2,1,0:T(8,128)(2,1)S(1)}, u32[]{:S(2)}, u32[]{:S(2)}) %collective-permute-start.1) | collective-permute-done | bytes 262176 | tf_op jit(solution)/shard_map/ppermute | solution.py:301
  282.4 0.0 collective-permute-done
  282.4 0.1 pad_maximum_fusion
  282.5 1.6 gather_fusion
  284.1 0.0 all-to-all-done.10
  284.1 0.0 copy-start.1
  284.1 0.7 copy-done.1
  284.8 17.0 %mix.1.mix_ref = f32[128,128]{1,0:T(8,128)} custom-call(f32[4,8,16,128]{3,2,1,0:T(8,128)} %bitcast.26, bf16[4,8,32,512]{3,2,1,0:T(8,128)(2,1)} %gather_fusion), custom_call_target="tpu_custom_call" | custom-call | tf_op jit(solution)/shard_map/mix/pallas_call | solution.py:241
  301.9 8.1 %merge.1 = bf16[896,4096]{1,0:T(8,128)(2,1)} custom-call(f32[128,128]{1,0:T(8,128)} %mix.1.mix_ref, bf16[4,32,896]{2,1,0:T(8,128)(2,1)} %all_to_all.63.in_ref.p_ref, bf16[4,8,32,512]{3,2,1,0:T(8,128)(2,1)} %gather_fusion), custom_call_target="tpu_custom_call" | custom-call | tf_op jit(solution)/shard_map/merge/pallas_call | solution.py:269
  (3 shorter events, 0.0 us)
Async XLA Ops:
  225.0 40.6 %copy-start = (bf16[8,32,512]{2,1,0:T(8,128)(2,1)S(1)}, bf16[8,32,512]{2,1,0:T(8,128)(2,1)}, u32[]{:S(2)}) copy-start(bf16[8,32,512]{2,1,0:T(8,128)(2,1)} %all_to_all.62.x_ref) | copy-start | bytes 786436
  262.9 21.2 %all-to-all-start.10 = ((f32[32,16,128]{2,1,0:T(8,128)}), f32[32,16,128]{2,1,0:T(8,128)S(1)}, u32[]{:S(2)}, u32[]{:S(2)}) async-start(f32[32,16,128]{2,1,0:T(8,128)} %broadcast_in_dim.14), calls=%async_computation.10 | async-start | bytes 524288 | tf_op jit(solution)/shard_map/all_to_all | solution.py:286
  265.6 9.8 %collective-permute-start.2 = (bf16[8,32,512]{2,1,0:T(8,128)(2,1)S(1)}, bf16[8,32,512]{2,1,0:T(8,128)(2,1)S(1)}, u32[]{:S(2)}, u32[]{:S(2)}) collective-permute-start(bf16[8,32,512]{2,1,0:T(8,128)(2,1)S(1)} %copy-done), channel_id=1, source_target_pairs={{0,24},{8,0},{16,8},{24,16},{1,25},{9,1},{17,9},{25,17},{2,26},{10... | collective-permute-start | bytes 786440 | tf_op jit(solution)/shard_map/ppermute | solution.py:301
  267.0 15.4 %collective-permute-start.1 = (bf16[8,32,512]{2,1,0:T(8,128)(2,1)S(1)}, bf16[8,32,512]{2,1,0:T(8,128)(2,1)S(1)}, u32[]{:S(2)}, u32[]{:S(2)}) collective-permute-start(bf16[8,32,512]{2,1,0:T(8,128)(2,1)S(1)} %copy-done), channel_id=1, source_target_pairs={{0,16},{8,24},{16,0},{24,8},{1,17},{9,25},{17,1},{25,9},{2,18},{10... | collective-permute-start | bytes 786440 | tf_op jit(solution)/shard_map/ppermute | solution.py:301
  267.3 15.1 %collective-permute-start = (bf16[8,32,512]{2,1,0:T(8,128)(2,1)S(1)}, bf16[8,32,512]{2,1,0:T(8,128)(2,1)S(1)}, u32[]{:S(2)}, u32[]{:S(2)}) collective-permute-start(bf16[8,32,512]{2,1,0:T(8,128)(2,1)S(1)} %copy-done), channel_id=1, source_target_pairs={{0,8},{8,16},{16,24},{24,0},{1,9},{9,17},{17,25},{25,1},{2,10},{10... | collective-permute-start | bytes 786440 | tf_op jit(solution)/shard_map/ppermute | solution.py:301
  284.1 0.7 copy-start.1

commit v2 on v0

v2 whole, which is shorter than its diff:
```python
import functools

import jax
import jax.numpy as jnp
from jax import lax
from jax.experimental import pallas as pl
from jax.experimental.pallas import tpu as pltpu
from jax.sharding import PartitionSpec as P

ITERS = 4
ROOT_STEPS = 12
HALVES = 2
LANES = 128
F32 = jnp.float32
BF16 = jnp.bfloat16
ROWS_BY_ROWS = (((1,), (1,)), ((), ()))
VMEM_BYTES = 26 * 1024 * 1024
IN_VMEM = pl.BlockSpec(memory_space=pltpu.VMEM)


def params():
    return pltpu.CompilerParams(vmem_limit_bytes=VMEM_BYTES)


def cost(flops, moved):
    return pl.CostEstimate(flops=flops, bytes_accessed=moved, transcendentals=0)


def split_two(value):
    high = value.astype(BF16)
    return high, (value - high.astype(F32)).astype(BF16)


def split_three(value):
    high = value.astype(BF16)
    rest = value - high.astype(F32)
    middle = rest.astype(BF16)
    return high, middle, (rest - middle.astype(F32)).astype(BF16)


def spread(value, order, axis):
    pieces = split_three(value)
    return jnp.concatenate([pieces[at] for at in order], axis=axis)


def square(left, right):
    return jnp.dot(
        spread(left, (0, 0, 1, 0, 2, 1), 1), spread(right, (0, 1, 0, 2, 0, 1), 0), preferred_element_type=F32
    )


def eye_of(size):
    return lax.broadcasted_iota(jnp.int32, (size, size), 0) == lax.broadcasted_iota(jnp.int32, (size, size), 1)


def lower_inverse(grams):
    size = grams[0].shape[0]
    rows = lax.broadcasted_iota(jnp.int32, (size, 1), 0)
    eye = eye_of(size).astype(F32)
    work = [jnp.concatenate([gram, eye], axis=1) for gram in grams]
    scale = [jnp.zeros((size, 1), F32) for _ in grams]
    for step in range(0, size, 2):
        after = step + 1
        for at, now in enumerate(work):
            first, second = now[step:after, :], now[after : after + 1, :]
            pivot, beside = now[step:after, step:after], now[step:after, after : after + 1]
            inverse = 1.0 / pivot
            ratio = beside * inverse
            second = second - ratio * first
            below = now[after : after + 1, after : after + 1] - ratio * beside
            col, col_after = now[:, step:after], now[:, after : after + 1]
            scale[at] = jnp.where(rows == step, lax.rsqrt(pivot), scale[at])
            scale[at] = jnp.where(rows == after, lax.rsqrt(below), scale[at])
            work[at] = (
                now
                - jnp.where(rows > step, col, 0.0) * (first * inverse)
                - jnp.where(rows > after, col_after - col * ratio, 0.0) * (second * (1.0 / below))
            )
    return [now[:, size:] * down for now, down in zip(work, scale)]


def tall_of(rows, *sizes):
    return next(size for size in (*sizes, rows) if rows % size == 0)


def first_kernel(tall, x_ref, d_ref, held_ref, out_ref, start, wide, sems, start_sem):
    count = d_ref.shape[0] // tall

    def copy(at):
        span = pl.ds(pl.multiple_of(at * tall, tall), tall)
        return pltpu.make_async_copy(d_ref.at[span], held_ref.at[span], sems.at[at])

    start_copy = pltpu.make_async_copy(x_ref, start, start_sem)
    start_copy.start()
    for at in range(count):
        copy(at).start()
    start_copy.wait()
    wide[...] = start[...].astype(BF16)

    def body(at, carry):
        copy(at).wait()
        span = pl.ds(pl.multiple_of(at * tall, tall), tall)
        out_ref[:, span] = lax.dot_general(
            wide[...], held_ref[span, :], ROWS_BY_ROWS, preferred_element_type=F32
        ).astype(BF16)
        return carry

    lax.fori_loop(0, count, body, 0)


def first(delta, start):
    rows, cols = delta.shape
    rank = start.shape[0]
    tall = tall_of(rows, 256, 128)
    return pl.pallas_call(
        functools.partial(first_kernel, tall),
        out_shape=(pltpu.VMEM((rows, cols), BF16), jax.ShapeDtypeStruct((rank, rows), BF16)),
        in_specs=[pl.BlockSpec(memory_space=pl.ANY)] * 2,
        out_specs=(IN_VMEM, IN_VMEM),
        scratch_shapes=[
            pltpu.VMEM((rank, cols), F32),
            pltpu.VMEM((rank, cols), BF16),
            pltpu.SemaphoreType.DMA((rows // tall,)),
            pltpu.SemaphoreType.DMA,
        ],
        cost_estimate=cost(2 * rows * cols * rank, 2 * rows * cols),
        compiler_params=params(),
        name="first",
    )(start, delta)


def backs_kernel(half, across, with_gram, images_ref, d_ref, _, out_ref):
    parts, rank, wide = out_ref.shape
    chunk = wide - LANES if with_gram else wide
    skip = wide - chunk
    images = images_ref[...]
    if with_gram:
        gram = lax.dot_general(images, images, ROWS_BY_ROWS, preferred_element_type=F32)
        spare = jnp.zeros((rank, LANES - 3 * rank), BF16)
        pieces = jnp.concatenate([*split_three(gram), spare], axis=1)
        for part in range(parts):
            out_ref[part, :, :skip] = pieces

    def body(at, carry):
        span = pl.ds(pl.multiple_of(half * parts * chunk + at * across, across), across)
        total = jnp.dot(images_ref[...], d_ref[:, span], preferred_element_type=F32).astype(BF16)
        for inner in range(across // chunk):
            out_ref[at * (across // chunk) + inner, :, skip:] = total[:, inner * chunk : (inner + 1) * chunk]
        return carry

    lax.fori_loop(0, parts * chunk // across, body, 0)


def backs(held, images, half, parts, with_gram):
    rows, cols = held.shape
    rank = images.shape[0]
    chunk = cols // HALVES // parts
    return pl.pallas_call(
        functools.partial(backs_kernel, half, max(chunk, 512), with_gram),
        out_shape=(
            pltpu.VMEM(held.shape, BF16),
            jax.ShapeDtypeStruct((parts, rank, chunk + (LANES if with_gram else 0)), BF16),
        ),
        in_specs=[IN_VMEM, IN_VMEM],
        out_specs=(IN_VMEM, IN_VMEM),
        input_output_aliases={1: 0},
        cost_estimate=cost(2 * rows * cols // HALVES * rank, 2 * rows * cols // HALVES),
        compiler_params=params(),
        name="backs",
    )(images, held)


def settle_first_kernel(in_ref, held_ref, after_ref, _, out_ref, lower_ref):
    parts, rank, wide = in_ref.shape
    total = in_ref[0].astype(F32)
    for part in range(1, parts):
        total = total + in_ref[part].astype(F32)
    gram = total[:, :rank] + total[:, rank : 2 * rank] + total[:, 2 * rank : 3 * rank]
    lower = lower_inverse([gram])[0]
    lower_ref[...] = lower
    block = square(lower, total[:, LANES:]).astype(BF16)
    for part in range(parts):
        out_ref[part] = block


def settle_next_kernel(in_ref, held_ref, lower_ref, _, out_ref):
    parts = in_ref.shape[0]
    total = in_ref[0].astype(F32)
    for part in range(1, parts):
        total = total + in_ref[part].astype(F32)
    block = square(lower_ref[...], total).astype(BF16)
    for part in range(parts):
        out_ref[part] = block


def settle_first(held, pieces, after):
    parts, rank, wide = pieces.shape
    return pl.pallas_call(
        settle_first_kernel,
        out_shape=(
            pltpu.VMEM(held.shape, BF16),
            jax.ShapeDtypeStruct((parts, rank, wide - LANES), BF16),
            jax.ShapeDtypeStruct((rank, rank), F32),
        ),
        in_specs=[IN_VMEM, IN_VMEM, pl.BlockSpec(memory_space=pl.ANY)],
        out_specs=(IN_VMEM, IN_VMEM, IN_VMEM),
        input_output_aliases={1: 0},
        cost_estimate=cost(10**8, 4 * 10**6),
        compiler_params=params(),
        name="settle_first",
    )(pieces, held, after)


def settle_next(held, pieces, lower):
    return pl.pallas_call(
        settle_next_kernel,
        out_shape=(pltpu.VMEM(held.shape, BF16), jax.ShapeDtypeStruct(pieces.shape, BF16)),
        in_specs=[IN_VMEM, IN_VMEM, IN_VMEM],
        out_specs=(IN_VMEM, IN_VMEM),
        input_output_aliases={1: 0},
        cost_estimate=cost(10**8, 2 * 10**6),
        compiler_params=params(),
        name="settle_next",
    )(pieces, held, lower)


def images_kernel(half, tall, partial, *refs):
    x_ref, d_ref = refs[:2]
    _, out_ref, wide, flat = refs[-4:]
    parts, _, chunk = x_ref.shape
    for part in range(parts):
        wide[:, part * chunk : (part + 1) * chunk] = x_ref[part]
    width = parts * chunk
    target = out_ref if len(out_ref.shape) == 2 else flat

    def body(at, carry):
        span = pl.ds(pl.multiple_of(at * tall, tall), tall)
        product = lax.dot_general(
            wide[...], d_ref[span, half * width : (half + 1) * width], ROWS_BY_ROWS, preferred_element_type=F32
        )
        if partial:
            product = product + refs[2][:, span]
        target[:, span] = product.astype(target.dtype)
        return carry

    lax.fori_loop(0, d_ref.shape[0] // tall, body, 0)
    if target is flat:
        each = out_ref.shape[2]
        for at in range(out_ref.shape[0]):
            out_ref[at] = flat[:, at * each : (at + 1) * each]


def images(held, block, half, partial=None, pieces=None):
    rows, cols = held.shape
    rank = block.shape[1]
    tall = tall_of(rows, 512, 896, 256, 128)
    shape = (rank, rows) if pieces is None else (pieces, rank, rows // pieces)
    operands = (block, held) if partial is None else (block, held, partial)
    return pl.pallas_call(
        functools.partial(images_kernel, half, tall, partial is not None),
        out_shape=(pltpu.VMEM(held.shape, BF16), jax.ShapeDtypeStruct(shape, F32 if partial is None else BF16)),
        in_specs=[IN_VMEM] * len(operands),
        out_specs=(IN_VMEM, IN_VMEM),
        input_output_aliases={1: 0},
        scratch_shapes=[pltpu.VMEM((rank, cols // HALVES), BF16), pltpu.VMEM((rank, rows), BF16)],
        cost_estimate=cost(2 * rows * cols // HALVES * rank, 2 * rows * cols // HALVES),
        compiler_params=params(),
        name="images",
    )(*operands)


def gram_kernel(in_ref, out_ref):
    flat = in_ref[...].reshape(-1, in_ref.shape[2])
    out_ref[...] = lax.dot_general(flat, flat, ROWS_BY_ROWS, preferred_element_type=F32).reshape(out_ref.shape)


def left_partial(panel, parts):
    tasks, rank, _ = panel.shape
    size = tasks * rank
    return pl.pallas_call(
        gram_kernel,
        out_shape=jax.ShapeDtypeStruct((parts, size // parts, size), F32),
        in_specs=[IN_VMEM],
        out_specs=IN_VMEM,
        compiler_params=params(),
        name="left_partial",
    )(panel)


def inverse_root(gram):
    identity = eye_of(gram.shape[0]).astype(F32)
    norm = jnp.sqrt(jnp.sum(gram * gram))

    def step(_, state):
        upper, lower = state
        middle = 0.5 * (3.0 * identity - square(lower, upper))
        return square(upper, middle), square(middle, lower)

    _, lower = lax.fori_loop(0, ROOT_STEPS, step, (gram / norm, identity))
    return lower / jnp.sqrt(norm)


def right_kernel(masks, parts, own_ref, *refs):
    blocks, (wide_ref, lower_ref, right_ref) = refs[:-3], refs[-3:]
    rank, chunk = blocks[0].shape[1:]
    tasks = len(masks)
    size = tasks * rank
    own = own_ref[0]
    for at, block in enumerate(blocks):
        half, place = divmod(at, tasks)
        down = pl.ds(pl.multiple_of(lax.bitwise_xor(own, masks[place]) * rank, rank), rank)
        for part in range(parts):
            left = (half * parts + part) * chunk
            wide_ref[down, left : left + chunk] = block[part]
    wide = wide_ref[...]
    raw = lax.dot_general(wide, wide, ROWS_BY_ROWS, preferred_element_type=F32)
    spans = [slice(task * rank, (task + 1) * rank) for task in range(tasks)]
    lower_ref[...] = jnp.zeros_like(lower_ref)
    for span, inverse in zip(spans, lower_inverse([raw[span, span] for span in spans])):
        lower_ref[span, span] = inverse
    lower = lower_ref[...]
    root = inverse_root(square(square(lower, raw), lower.T))
    right_ref[...] = square(root.T, lower)


def right(own, blocks, masks):
    parts, rank, chunk = blocks[0].shape
    size = len(masks) * rank
    return pl.pallas_call(
        functools.partial(right_kernel, masks, parts),
        out_shape=(
            jax.ShapeDtypeStruct((size, HALVES * parts * chunk), BF16),
            jax.ShapeDtypeStruct((size, size), F32),
            jax.ShapeDtypeStruct((size, size), F32),
        ),
        in_specs=[pl.BlockSpec(memory_space=pltpu.SMEM)] + [IN_VMEM] * len(blocks),
        out_specs=(IN_VMEM,) * 3,
        cost_estimate=cost(10**10, 10**6),
        compiler_params=params(),
        name="right",
    )(own, *blocks)


def finish_kernel(tasks, gram_ref, panel_ref, wide_ref, lower_ref, right_ref, out_ref, side):
    size = lower_ref.shape[0]

    @pl.when(pl.program_id(0) == 0)
    def _():
        raw = gram_ref[0]
        for task in range(1, tasks):
            raw = raw + gram_ref[task]
        raw = raw.reshape(size, size)
        lower = lower_ref[...]
        gram = square(square(lower, raw), lower.T)
        diagonal = jnp.where(eye_of(size), gram, 0.0)
        down = jnp.sqrt(jnp.sum(diagonal, axis=1, keepdims=True))
        across = jnp.sqrt(jnp.sum(diagonal, axis=0, keepdims=True))
        mixing = inverse_root(gram / (down * across)) / down * across
        mixed = square(square(lower.T, mixing), right_ref[...])
        panel = panel_ref[...].reshape(size, panel_ref.shape[2]).T
        product = jnp.dot(
            jnp.concatenate([panel, panel], axis=1),
            jnp.concatenate(split_two(mixed), axis=0),
            preferred_element_type=F32,
        )
        side[...] = jnp.concatenate(split_two(product), axis=1)

    wide = wide_ref[...]
    out_ref[...] = jnp.dot(
        side[...], jnp.concatenate([wide, wide], axis=0), preferred_element_type=F32
    ).astype(BF16)


def finish(grams, panel, wide, lower, right_side):
    tasks, parts, each, size = grams.shape
    rows, cols = panel.shape[2], wide.shape[1]
    across = 512

    def whole(shape):
        return pl.BlockSpec(shape, lambda at: (0,) * len(shape))

    return pl.pallas_call(
        functools.partial(finish_kernel, tasks),
        out_shape=jax.ShapeDtypeStruct((rows, cols), BF16),
        grid=(cols // across,),
        in_specs=[
            whole(grams.shape),
            whole(panel.shape),
            pl.BlockSpec((size, across), lambda at: (0, at)),
            whole(lower.shape),
            whole(right_side.shape),
        ],
        out_specs=pl.BlockSpec((rows, across), lambda at: (0, at)),
        scratch_shapes=[pltpu.VMEM((rows, 2 * size), BF16)],
        compiler_params=params(),
        name="finish",
    )(grams, panel, wide, lower, right_side)


def swap(pieces, axis):
    return lax.all_to_all(pieces, axis, split_axis=0, concat_axis=0, tiled=True)


def spread_over_tasks(block, tasks):
    masks, blocks = [0], [block]
    bit = tasks // 2
    while bit:
        pairs = [(at, at ^ bit) for at in range(tasks)]
        blocks = blocks + [lax.ppermute(each, "task", pairs) for each in blocks]
        masks = masks + [mask ^ bit for mask in masks]
        bit //= 2
    return tuple(masks), blocks


def local(tasks, parts, task_delta, start_block):
    held, panel = first(task_delta[0], start_block[0].T)
    for step in range(ITERS):
        held, near = backs(held, panel, 0, parts, True)
        held, far = backs(held, panel, 1, parts, False)
        held, near, lower = settle_first(held, swap(near, "row"), far)
        near = swap(near, "row")
        held, far = settle_next(held, swap(far, "row"), lower)
        far = swap(far, "row")
        held, panel = images(held, near, 0)
        held, panel = images(held, far, 1, panel, tasks if step == ITERS - 1 else None)
    masks, near_all = spread_over_tasks(near, tasks)
    _, far_all = spread_over_tasks(far, tasks)
    panel = swap(panel, "task")
    partial = jnp.sum(swap(left_partial(panel, parts), "row"), axis=0)
    grams = swap(jnp.broadcast_to(partial[None], (tasks * parts, *partial.shape)), ("task", "row"))
    own = lax.axis_index("task").astype(jnp.int32).reshape(1)
    wide, lower, right_side = right(own, near_all + far_all, masks)
    return finish(grams.reshape(tasks, parts, *partial.shape), panel, wide, lower, right_side)


def solution(mesh):
    tasks, parts = mesh.shape["task"], mesh.shape["row"]
    placed = (P("task", "row", None), P("task", None, None))
    return jax.shard_map(
        functools.partial(local, tasks, parts),
        mesh=mesh,
        in_specs=placed,
        out_specs=P(("row", "task"), None),
        check_vma=False,
    )
```

time: 668 us -> 686 us (1.027)
  waiting for transfers between devices: 417 us -> 15.6 us
  local copies, waits for them, and re-layouts: 2.26 us -> 385 us
  matrix products: 188 us -> 0 us
  Pallas kernels: 0 us -> 171 us
  starting transfers between devices: 0.6 us -> 112 us
  other arithmetic: 28.4 us -> 0.01 us
  between operations: 16.1 us -> 0.32 us
  blocking collectives: 8.22 us -> 0 us
    psum x5 -> x0, waiting for transfers between devices: 406 us -> none  [the longest x4 290 us: local(): backs = lax.psum(partial_value, 'row')]
    unnamed x2 -> x116, local copies, waits for them, and re-layouts: 0.01 us -> 384 us
    dot_general x84 -> x0, matrix products: 182 us -> none  [the longest x4 120 us: local(): lax.dot_general(local_rows, images, (((0,), (0,)), ((), ())), preferred_e...]
    pallas_call x0 -> x28, Pallas kernels: none -> 171 us  [the longest x8 55 us: images(): pl.pallas_call(functools.partial(images_kernel, half, tall, partial is no...]
    all_to_all x0 -> x19, starting transfers between devices: none -> 109 us  [swap(): return lax.all_to_all(pieces, axis, split_axis=0, concat_axis=0, tiled=True)]
    another operation x21 -> x0, other arithmetic: 26.7 us -> none  [the longest x12 14.4 us: orthonormal(): factor = jnp.linalg.cholesky(gram)]
    all_gather x1 -> x0, waiting for transfers between devices: 11.2 us -> none  [local(): bases = lax.all_gather(current, 'task', axis=1, tiled=True)]
    ppermute x0 -> x6, waiting for transfers between devices: none -> 8.66 us  [spread_over_tasks(): blocks = blocks + [lax.ppermute(each, 'task', pairs) for each in blocks]]
  transfers between devices with their start and end apart: 6 -> 25, of which waited for: 6 -> 3; matrix products, arithmetic and copies ran while one was open for 2% -> 0% of each run, Pallas kernels for 0% -> 13%
where the time goes in v2:
time: 686 us; the launch traced here: 683 us
  local copies, waits for them, and re-layouts  385 us (56%)
  Pallas kernels  171 us (25%)
  starting transfers between devices  112 us (16%)
  waiting for transfers between devices  15.6 us (2%)
    unnamed x116, local copies, waits for them, and re-layouts  384 us
    all_to_all x19, starting transfers between devices, swap(): return lax.all_to_all(pieces, axis, split_axis=0, concat_axis=0, tiled=True)  109 us
    pallas_call x8, Pallas kernels, images(): pl.pallas_call(functools.partial(images_kernel, half, tall, partial is no...  55 us
    pallas_call x8, Pallas kernels, backs(): pl.pallas_call(functools.partial(backs_kernel, half, max(chunk, 512), wit...  37.5 us
    pallas_call x4, Pallas kernels, settle_first(): pl.pallas_call(settle_first_kernel, out_shape=(pltpu.VMEM(held.shape, BF1...  25.4 us
    pallas_call x1, Pallas kernels, first(): pl.pallas_call(functools.partial(first_kernel, tall), out_shape=(pltpu.VM...  20 us
  transfers between devices with their start and end apart: 25, of which 3 were waited for; matrix products, arithmetic and copies ran while one was open for 0% of the time, Pallas kernels for 13%

profile of v2, /device:TPU:0, one launch (start us, length us, event | category | flops | bytes accessed | tf_op | source)
XLA Modules:
  0.0 683.1 jit_solution(3361256545715916869)
XLA Ops:
  0.0 20.0 %first.1 = (bf16[3584,4096]{1,0:T(8,128)(2,1)S(1)}, bf16[32,3584]{1,0:T(8,128)(2,1)}) custom-call(f32[32,4096]{1,0:T(8,128)} %bitcast.8, bf16[3584,4096]{1,0:T(8,128)(2,1)} %bitcast.7), custom_call_target="tpu_custom_call" | custom-call | flops 939524096 | bytes 29360128 | tf_op jit(solution)/shard_map/first/pallas_call | solution.py:115
  24.8 9.7 %copy-done = bf16[3584,4096]{1,0:T(8,128)(2,1)} copy-done((bf16[3584,4096]{1,0:T(8,128)(2,1)}, bf16[3584,4096]{1,0:T(8,128)(2,1)S(1)}, u32[]{:S(2)}) %copy-start) | copy-done | bytes 29360152
  34.5 7.3 %all-to-all-start.1 = ((bf16[8,32,384]{2,1,0:T(8,128)(2,1)}), bf16[8,32,384]{2,1,0:T(8,128)(2,1)S(1)}, u32[]{:S(2)}, u32[]{:S(2)}) async-start(bf16[8,32,384]{2,1,0:T(8,128)(2,1)} %get-tuple-element.65), calls=%async_computation.1 | async-start | bytes 393216 | tf_op jit(solution)/shard_map/all_to_all | solution.py:401
  41.8 9.3 %copy-done.1 = bf16[3584,4096]{1,0:T(8,128)(2,1)S(1)} copy-done((bf16[3584,4096]{1,0:T(8,128)(2,1)S(1)}, bf16[3584,4096]{1,0:T(8,128)(2,1)}, u32[]{:S(2)}) %copy-start.1) | copy-done | bytes 29360152
  55.7 9.7 %copy-done.2 = bf16[3584,4096]{1,0:T(8,128)(2,1)} copy-done((bf16[3584,4096]{1,0:T(8,128)(2,1)}, bf16[3584,4096]{1,0:T(8,128)(2,1)S(1)}, u32[]{:S(2)}) %copy-start.2) | copy-done | bytes 29360152
  65.4 6.0 all-to-all-start
  71.4 9.3 %copy-done.3 = bf16[3584,4096]{1,0:T(8,128)(2,1)S(1)} copy-done((bf16[3584,4096]{1,0:T(8,128)(2,1)S(1)}, bf16[3584,4096]{1,0:T(8,128)(2,1)}, u32[]{:S(2)}) %copy-start.3) | copy-done | bytes 29360152
  80.7 6.4 settle_first.4
  87.1 9.7 %copy-done.4 = bf16[3584,4096]{1,0:T(8,128)(2,1)} copy-done((bf16[3584,4096]{1,0:T(8,128)(2,1)}, bf16[3584,4096]{1,0:T(8,128)(2,1)S(1)}, u32[]{:S(2)}) %copy-start.4) | copy-done | bytes 29360152
  96.8 6.0 all-to-all-start.3
  102.8 9.3 %copy-done.5 = bf16[3584,4096]{1,0:T(8,128)(2,1)S(1)} copy-done((bf16[3584,4096]{1,0:T(8,128)(2,1)S(1)}, bf16[3584,4096]{1,0:T(8,128)(2,1)}, u32[]{:S(2)}) %copy-start.5) | copy-done | bytes 29360152
  113.9 9.7 %copy-done.6 = bf16[3584,4096]{1,0:T(8,128)(2,1)} copy-done((bf16[3584,4096]{1,0:T(8,128)(2,1)}, bf16[3584,4096]{1,0:T(8,128)(2,1)S(1)}, u32[]{:S(2)}) %copy-start.6) | copy-done | bytes 29360152
  123.6 6.0 all-to-all-start.2
  129.6 9.3 %copy-done.7 = bf16[3584,4096]{1,0:T(8,128)(2,1)S(1)} copy-done((bf16[3584,4096]{1,0:T(8,128)(2,1)S(1)}, bf16[3584,4096]{1,0:T(8,128)(2,1)}, u32[]{:S(2)}) %copy-start.7) | copy-done | bytes 29360152
  138.9 6.8 images.8
  145.8 9.7 %copy-done.8 = bf16[3584,4096]{1,0:T(8,128)(2,1)} copy-done((bf16[3584,4096]{1,0:T(8,128)(2,1)}, bf16[3584,4096]{1,0:T(8,128)(2,1)S(1)}, u32[]{:S(2)}) %copy-start.8) | copy-done | bytes 29360152
  156.1 9.3 %copy-done.9 = bf16[3584,4096]{1,0:T(8,128)(2,1)S(1)} copy-done((bf16[3584,4096]{1,0:T(8,128)(2,1)S(1)}, bf16[3584,4096]{1,0:T(8,128)(2,1)}, u32[]{:S(2)}) %copy-start.9) | copy-done | bytes 29360152
  165.4 6.9 %images.9 = (bf16[3584,4096]{1,0:T(8,128)(2,1)S(1)}, bf16[32,3584]{1,0:T(8,128)(2,1)}) custom-call(bf16[8,32,256]{2,1,0:T(8,128)(2,1)} %copy-done.55, bf16[3584,4096]{1,0:T(8,128)(2,1)S(1)} %copy-done.9, f32[32,3584]{1,0:T(8,128)} %get-tuple-element.73.refs_2_), custom_call_target="tpu_custom_call", output_to_operand_aliasing={{0}: (1, {})} | custom-call | flops 469762048 | bytes 14680064 | tf_op jit(solution)/shard_map/images/pallas_call | solution.py:259
  177.2 9.7 %copy-done.10 = bf16[3584,4096]{1,0:T(8,128)(2,1)} copy-done((bf16[3584,4096]{1,0:T(8,128)(2,1)}, bf16[3584,4096]{1,0:T(8,128)(2,1)S(1)}, u32[]{:S(2)}) %copy-start.10) | copy-done | bytes 29360152
  192.9 9.3 %copy-done.11 = bf16[3584,4096]{1,0:T(8,128)(2,1)S(1)} copy-done((bf16[3584,4096]{1,0:T(8,128)(2,1)S(1)}, bf16[3584,4096]{1,0:T(8,128)(2,1)}, u32[]{:S(2)}) %copy-start.11) | copy-done | bytes 29360152
  206.8 9.7 %copy-done.12 = bf16[3584,4096]{1,0:T(8,128)(2,1)} copy-done((bf16[3584,4096]{1,0:T(8,128)(2,1)}, bf16[3584,4096]{1,0:T(8,128)(2,1)S(1)}, u32[]{:S(2)}) %copy-start.12) | copy-done | bytes 29360152
  216.5 6.0 all-to-all-start.4
  222.5 9.3 %copy-done.13 = bf16[3584,4096]{1,0:T(8,128)(2,1)S(1)} copy-done((bf16[3584,4096]{1,0:T(8,128)(2,1)S(1)}, bf16[3584,4096]{1,0:T(8,128)(2,1)}, u32[]{:S(2)}) %copy-start.13) | copy-done | bytes 29360152
  231.8 6.4 settle_first.5
  238.2 9.7 %copy-done.14 = bf16[3584,4096]{1,0:T(8,128)(2,1)} copy-done((bf16[3584,4096]{1,0:T(8,128)(2,1)}, bf16[3584,4096]{1,0:T(8,128)(2,1)S(1)}, u32[]{:S(2)}) %copy-start.14) | copy-done | bytes 29360152
  253.9 9.3 %copy-done.15 = bf16[3584,4096]{1,0:T(8,128)(2,1)S(1)} copy-done((bf16[3584,4096]{1,0:T(8,128)(2,1)S(1)}, bf16[3584,4096]{1,0:T(8,128)(2,1)}, u32[]{:S(2)}) %copy-start.15) | copy-done | bytes 29360152
  265.0 9.7 %copy-done.16 = bf16[3584,4096]{1,0:T(8,128)(2,1)} copy-done((bf16[3584,4096]{1,0:T(8,128)(2,1)}, bf16[3584,4096]{1,0:T(8,128)(2,1)S(1)}, u32[]{:S(2)}) %copy-start.16) | copy-done | bytes 29360152
  280.7 9.3 %copy-done.17 = bf16[3584,4096]{1,0:T(8,128)(2,1)S(1)} copy-done((bf16[3584,4096]{1,0:T(8,128)(2,1)S(1)}, bf16[3584,4096]{1,0:T(8,128)(2,1)}, u32[]{:S(2)}) %copy-start.17) | copy-done | bytes 29360152
  290.0 6.8 images.10
  296.8 9.7 %copy-done.18 = bf16[3584,4096]{1,0:T(8,128)(2,1)} copy-done((bf16[3584,4096]{1,0:T(8,128)(2,1)}, bf16[3584,4096]{1,0:T(8,128)(2,1)S(1)}, u32[]{:S(2)}) %copy-start.18) | copy-done | bytes 29360152
  307.2 9.3 %copy-done.19 = bf16[3584,4096]{1,0:T(8,128)(2,1)S(1)} copy-done((bf16[3584,4096]{1,0:T(8,128)(2,1)S(1)}, bf16[3584,4096]{1,0:T(8,128)(2,1)}, u32[]{:S(2)}) %copy-start.19) | copy-done | bytes 29360152
  316.5 6.9 %images.11 = (bf16[3584,4096]{1,0:T(8,128)(2,1)S(1)}, bf16[32,3584]{1,0:T(8,128)(2,1)}) custom-call(bf16[8,32,256]{2,1,0:T(8,128)(2,1)} %copy-done.56, bf16[3584,4096]{1,0:T(8,128)(2,1)S(1)} %copy-done.19, f32[32,3584]{1,0:T(8,128)} %get-tuple-element.86.refs_2_), custom_call_target="tpu_custom_call", output_to_operand_aliasing={{0}: (1, {})} | custom-call | flops 469762048 | bytes 14680064 | tf_op jit(solution)/shard_map/images/pallas_call | solution.py:259
  328.3 9.7 %copy-done.20 = bf16[3584,4096]{1,0:T(8,128)(2,1)} copy-done((bf16[3584,4096]{1,0:T(8,128)(2,1)}, bf16[3584,4096]{1,0:T(8,128)(2,1)S(1)}, u32[]{:S(2)}) %copy-start.20) | copy-done | bytes 29360152
  344.0 9.3 %copy-done.21 = bf16[3584,4096]{1,0:T(8,128)(2,1)S(1)} copy-done((bf16[3584,4096]{1,0:T(8,128)(2,1)S(1)}, bf16[3584,4096]{1,0:T(8,128)(2,1)}, u32[]{:S(2)}) %copy-start.21) | copy-done | bytes 29360152
  357.9 9.7 %copy-done.22 = bf16[3584,4096]{1,0:T(8,128)(2,1)} copy-done((bf16[3584,4096]{1,0:T(8,128)(2,1)}, bf16[3584,4096]{1,0:T(8,128)(2,1)S(1)}, u32[]{:S(2)}) %copy-start.22) | copy-done | bytes 29360152
  367.6 6.0 all-to-all-start.8
  373.6 9.3 %copy-done.23 = bf16[3584,4096]{1,0:T(8,128)(2,1)S(1)} copy-done((bf16[3584,4096]{1,0:T(8,128)(2,1)S(1)}, bf16[3584,4096]{1,0:T(8,128)(2,1)}, u32[]{:S(2)}) %copy-start.23) | copy-done | bytes 29360152
  382.9 6.4 settle_first.6
  389.3 9.7 %copy-done.24 = bf16[3584,4096]{1,0:T(8,128)(2,1)} copy-done((bf16[3584,4096]{1,0:T(8,128)(2,1)}, bf16[3584,4096]{1,0:T(8,128)(2,1)S(1)}, u32[]{:S(2)}) %copy-start.24) | copy-done | bytes 29360152
  405.0 9.3 %copy-done.25 = bf16[3584,4096]{1,0:T(8,128)(2,1)S(1)} copy-done((bf16[3584,4096]{1,0:T(8,128)(2,1)S(1)}, bf16[3584,4096]{1,0:T(8,128)(2,1)}, u32[]{:S(2)}) %copy-start.25) | copy-done | bytes 29360152
  416.1 9.7 %copy-done.26 = bf16[3584,4096]{1,0:T(8,128)(2,1)} copy-done((bf16[3584,4096]{1,0:T(8,128)(2,1)}, bf16[3584,4096]{1,0:T(8,128)(2,1)S(1)}, u32[]{:S(2)}) %copy-start.26) | copy-done | bytes 29360152
  431.8 9.3 %copy-done.27 = bf16[3584,4096]{1,0:T(8,128)(2,1)S(1)} copy-done((bf16[3584,4096]{1,0:T(8,128)(2,1)S(1)}, bf16[3584,4096]{1,0:T(8,128)(2,1)}, u32[]{:S(2)}) %copy-start.27) | copy-done | bytes 29360152
  441.1 6.8 images.12
  447.9 9.7 %copy-done.28 = bf16[3584,4096]{1,0:T(8,128)(2,1)} copy-done((bf16[3584,4096]{1,0:T(8,128)(2,1)}, bf16[3584,4096]{1,0:T(8,128)(2,1)S(1)}, u32[]{:S(2)}) %copy-start.28) | copy-done | bytes 29360152
  458.3 9.3 %copy-done.29 = bf16[3584,4096]{1,0:T(8,128)(2,1)S(1)} copy-done((bf16[3584,4096]{1,0:T(8,128)(2,1)S(1)}, bf16[3584,4096]{1,0:T(8,128)(2,1)}, u32[]{:S(2)}) %copy-start.29) | copy-done | bytes 29360152
  467.6 6.9 %images.13 = (bf16[3584,4096]{1,0:T(8,128)(2,1)S(1)}, bf16[32,3584]{1,0:T(8,128)(2,1)}) custom-call(bf16[8,32,256]{2,1,0:T(8,128)(2,1)} %copy-done.57, bf16[3584,4096]{1,0:T(8,128)(2,1)S(1)} %copy-done.29, f32[32,3584]{1,0:T(8,128)} %get-tuple-element.99.refs_2_), custom_call_target="tpu_custom_call", output_to_operand_aliasing={{0}: (1, {})} | custom-call | flops 469762048 | bytes 14680064 | tf_op jit(solution)/shard_map/images/pallas_call | solution.py:259
  479.4 9.7 %copy-done.30 = bf16[3584,4096]{1,0:T(8,128)(2,1)} copy-done((bf16[3584,4096]{1,0:T(8,128)(2,1)}, bf16[3584,4096]{1,0:T(8,128)(2,1)S(1)}, u32[]{:S(2)}) %copy-start.30) | copy-done | bytes 29360152
  495.1 9.3 %copy-done.31 = bf16[3584,4096]{1,0:T(8,128)(2,1)S(1)} copy-done((bf16[3584,4096]{1,0:T(8,128)(2,1)S(1)}, bf16[3584,4096]{1,0:T(8,128)(2,1)}, u32[]{:S(2)}) %copy-start.31) | copy-done | bytes 29360152
  509.0 9.7 %copy-done.32 = bf16[3584,4096]{1,0:T(8,128)(2,1)} copy-done((bf16[3584,4096]{1,0:T(8,128)(2,1)}, bf16[3584,4096]{1,0:T(8,128)(2,1)S(1)}, u32[]{:S(2)}) %copy-start.32) | copy-done | bytes 29360152
  518.7 6.0 all-to-all-start.12
  524.7 9.3 %copy-done.33 = bf16[3584,4096]{1,0:T(8,128)(2,1)S(1)} copy-done((bf16[3584,4096]{1,0:T(8,128)(2,1)S(1)}, bf16[3584,4096]{1,0:T(8,128)(2,1)}, u32[]{:S(2)}) %copy-start.33) | copy-done | bytes 29360152
  534.0 6.4 settle_first.7
  540.4 9.7 %copy-done.34 = bf16[3584,4096]{1,0:T(8,128)(2,1)} copy-done((bf16[3584,4096]{1,0:T(8,128)(2,1)}, bf16[3584,4096]{1,0:T(8,128)(2,1)S(1)}, u32[]{:S(2)}) %copy-start.34) | copy-done | bytes 29360152
  556.1 9.3 %copy-done.35 = bf16[3584,4096]{1,0:T(8,128)(2,1)S(1)} copy-done((bf16[3584,4096]{1,0:T(8,128)(2,1)S(1)}, bf16[3584,4096]{1,0:T(8,128)(2,1)}, u32[]{:S(2)}) %copy-start.35) | copy-done | bytes 29360152
  567.2 9.7 %copy-done.36 = bf16[3584,4096]{1,0:T(8,128)(2,1)} copy-done((bf16[3584,4096]{1,0:T(8,128)(2,1)}, bf16[3584,4096]{1,0:T(8,128)(2,1)S(1)}, u32[]{:S(2)}) %copy-start.36) | copy-done | bytes 29360152
  582.9 9.3 %copy-done.37 = bf16[3584,4096]{1,0:T(8,128)(2,1)S(1)} copy-done((bf16[3584,4096]{1,0:T(8,128)(2,1)S(1)}, bf16[3584,4096]{1,0:T(8,128)(2,1)}, u32[]{:S(2)}) %copy-start.37) | copy-done | bytes 29360152
  592.2 6.8 images.14
  599.0 9.7 %copy-done.38 = bf16[3584,4096]{1,0:T(8,128)(2,1)} copy-done((bf16[3584,4096]{1,0:T(8,128)(2,1)}, bf16[3584,4096]{1,0:T(8,128)(2,1)S(1)}, u32[]{:S(2)}) %copy-start.38) | copy-done | bytes 29360152
  609.4 9.3 %copy-done.39 = bf16[3584,4096]{1,0:T(8,128)(2,1)S(1)} copy-done((bf16[3584,4096]{1,0:T(8,128)(2,1)S(1)}, bf16[3584,4096]{1,0:T(8,128)(2,1)}, u32[]{:S(2)}) %copy-start.39) | copy-done | bytes 29360152
  618.7 7.0 %images.15 = (bf16[3584,4096]{1,0:T(8,128)(2,1)S(1)}, bf16[4,32,896]{2,1,0:T(8,128)(2,1)}) custom-call(bf16[8,32,256]{2,1,0:T(8,128)(2,1)} %copy-done.42, bf16[3584,4096]{1,0:T(8,128)(2,1)S(1)} %copy-done.39, f32[32,3584]{1,0:T(8,128)} %get-tuple-element.112.refs_2_), custom_call_target="tpu_custom_call", output_to_operand_aliasing={{0}: (1, {})} | custom-call | flops 469762048 | bytes 14680064 | tf_op jit(solution)/shard_map/images/pallas_call | solution.py:259
  631.7 6.3 collective-permute-done.refs_1_
  647.2 6.9 %all-to-all-done.17 = f32[8,16,128]{2,1,0:T(8,128)S(1)} async-done(((f32[8,16,128]{2,1,0:T(8,128)}), f32[8,16,128]{2,1,0:T(8,128)S(1)}, u32[]{:S(2)}, u32[]{:S(2)}) %all-to-all-start.17) | async-done | bytes 65568 | tf_op jit(solution)/shard_map/all_to_all | solution.py:401
  658.4 12.1 %right.1 = (bf16[128,4096]{1,0:T(8,128)(2,1)S(1)}, f32[128,128]{1,0:T(8,128)S(1)}, f32[128,128]{1,0:T(8,128)S(1)}) custom-call(s32[1]{0:T(128)} %bitcast.4.own_ref, bf16[8,32,256]{2,1,0:T(8,128)(2,1)S(1)} %copy-done.41, bf16[8,32,256]{2,1,0:T(8,128)(2,1)S(1)} %collective-permute-done.refs_1_, bf16[8,32,256]{2,1,0:T(8,128)(2,1)S(1)} %collective-permute-done.1.refs_2_, ...), custom_call_target="tpu_custom_call" | custom-call | flops 10000000000 | bytes 1000000 | tf_op jit(solution)/shard_map/right/pallas_call | solution.py:329
  670.5 12.6 %finish.1 = bf16[896,4096]{1,0:T(8,128)(2,1)} custom-call(f32[4,8,16,128]{3,2,1,0:T(8,128)S(1)} %bitcast.6, bf16[4,32,896]{2,1,0:T(8,128)(2,1)S(1)} %all-to-all-done.16.in_ref.panel_ref, bf16[128,4096]{1,0:T(8,128)(2,1)S(1)} %get-tuple-element.114.wide_ref, f32[128,128]{1,0:T(8,128)S(1)} %get-tuple-element.115.lower_ref, ...), custom_call_target="tpu_custom_call" | custom-call | tf_op jit(solution)/shard_map/finish/pallas_call | solution.py:382
  (132 shorter events, 120.6 us)
Async XLA Ops:
  24.8 9.7 %copy-start = (bf16[3584,4096]{1,0:T(8,128)(2,1)}, bf16[3584,4096]{1,0:T(8,128)(2,1)S(1)}, u32[]{:S(2)}) copy-start(bf16[3584,4096]{1,0:T(8,128)(2,1)S(1)} %get-tuple-element.63.d_ref) | copy-start | bytes 88080384
  34.5 30.9 %all-to-all-start.1 = ((bf16[8,32,384]{2,1,0:T(8,128)(2,1)}), bf16[8,32,384]{2,1,0:T(8,128)(2,1)S(1)}, u32[]{:S(2)}, u32[]{:S(2)}) async-start(bf16[8,32,384]{2,1,0:T(8,128)(2,1)} %get-tuple-element.65), calls=%async_computation.1 | async-start | bytes 393216 | tf_op jit(solution)/shard_map/all_to_all | solution.py:401
  41.8 9.4 %copy-start.1 = (bf16[3584,4096]{1,0:T(8,128)(2,1)S(1)}, bf16[3584,4096]{1,0:T(8,128)(2,1)}, u32[]{:S(2)}) copy-start(bf16[3584,4096]{1,0:T(8,128)(2,1)} %copy-done) | copy-start | bytes 88080384
  55.7 9.7 %copy-start.2 = (bf16[3584,4096]{1,0:T(8,128)(2,1)}, bf16[3584,4096]{1,0:T(8,128)(2,1)S(1)}, u32[]{:S(2)}) copy-start(bf16[3584,4096]{1,0:T(8,128)(2,1)S(1)} %get-tuple-element.66.held_ref) | copy-start | bytes 88080384
  65.4 31.4 %all-to-all-start = ((bf16[8,32,256]{2,1,0:T(8,128)(2,1)}), bf16[8,32,256]{2,1,0:T(8,128)(2,1)S(1)}, u32[]{:S(2)}, u32[]{:S(2)}) async-start(bf16[8,32,256]{2,1,0:T(8,128)(2,1)} %get-tuple-element.64.after_ref), calls=%async_computation | async-start | bytes 262144 | tf_op jit(solution)/shard_map/all_to_all | solution.py:401
  71.4 9.4 %copy-start.3 = (bf16[3584,4096]{1,0:T(8,128)(2,1)S(1)}, bf16[3584,4096]{1,0:T(8,128)(2,1)}, u32[]{:S(2)}) copy-start(bf16[3584,4096]{1,0:T(8,128)(2,1)} %copy-done.2) | copy-start | bytes 88080384
  87.1 9.7 %copy-start.4 = (bf16[3584,4096]{1,0:T(8,128)(2,1)}, bf16[3584,4096]{1,0:T(8,128)(2,1)S(1)}, u32[]{:S(2)}) copy-start(bf16[3584,4096]{1,0:T(8,128)(2,1)S(1)} %get-tuple-element.67.held_ref) | copy-start | bytes 88080384
  96.8 26.8 %all-to-all-start.3 = ((bf16[8,32,256]{2,1,0:T(8,128)(2,1)}), bf16[8,32,256]{2,1,0:T(8,128)(2,1)S(1)}, u32[]{:S(2)}, u32[]{:S(2)}) async-start(bf16[8,32,256]{2,1,0:T(8,128)(2,1)} %get-tuple-element.70), calls=%async_computation.3 | async-start | bytes 262144 | tf_op jit(solution)/shard_map/all_to_all | solution.py:401
  102.8 9.4 %copy-start.5 = (bf16[3584,4096]{1,0:T(8,128)(2,1)S(1)}, bf16[3584,4096]{1,0:T(8,128)(2,1)}, u32[]{:S(2)}) copy-start(bf16[3584,4096]{1,0:T(8,128)(2,1)} %copy-done.4) | copy-start | bytes 88080384
  113.9 9.7 %copy-start.6 = (bf16[3584,4096]{1,0:T(8,128)(2,1)}, bf16[3584,4096]{1,0:T(8,128)(2,1)S(1)}, u32[]{:S(2)}) copy-start(bf16[3584,4096]{1,0:T(8,128)(2,1)S(1)} %get-tuple-element.71.refs_1_) | copy-start | bytes 88080384
  123.6 31.8 %all-to-all-start.2 = ((bf16[8,32,256]{2,1,0:T(8,128)(2,1)}), bf16[8,32,256]{2,1,0:T(8,128)(2,1)S(1)}, u32[]{:S(2)}, u32[]{:S(2)}) async-start(bf16[8,32,256]{2,1,0:T(8,128)(2,1)} %get-tuple-element.69), calls=%async_computation.2 | async-start | bytes 262144 | tf_op jit(solution)/shard_map/all_to_all | solution.py:401
  129.6 9.4 %copy-start.7 = (bf16[3584,4096]{1,0:T(8,128)(2,1)S(1)}, bf16[3584,4096]{1,0:T(8,128)(2,1)}, u32[]{:S(2)}) copy-start(bf16[3584,4096]{1,0:T(8,128)(2,1)} %copy-done.6) | copy-start | bytes 88080384
  145.7 9.7 %copy-start.8 = (bf16[3584,4096]{1,0:T(8,128)(2,1)}, bf16[3584,4096]{1,0:T(8,128)(2,1)S(1)}, u32[]{:S(2)}) copy-start(bf16[3584,4096]{1,0:T(8,128)(2,1)S(1)} %get-tuple-element.72.refs_1_) | copy-start | bytes 88080384
  156.1 9.4 %copy-start.9 = (bf16[3584,4096]{1,0:T(8,128)(2,1)S(1)}, bf16[3584,4096]{1,0:T(8,128)(2,1)}, u32[]{:S(2)}) copy-start(bf16[3584,4096]{1,0:T(8,128)(2,1)} %copy-done.8) | copy-start | bytes 88080384
  177.2 9.7 %copy-start.10 = (bf16[3584,4096]{1,0:T(8,128)(2,1)}, bf16[3584,4096]{1,0:T(8,128)(2,1)S(1)}, u32[]{:S(2)}) copy-start(bf16[3584,4096]{1,0:T(8,128)(2,1)S(1)} %get-tuple-element.76.d_ref) | copy-start | bytes 88080384
  186.9 29.6 %all-to-all-start.5 = ((bf16[8,32,384]{2,1,0:T(8,128)(2,1)}), bf16[8,32,384]{2,1,0:T(8,128)(2,1)S(1)}, u32[]{:S(2)}, u32[]{:S(2)}) async-start(bf16[8,32,384]{2,1,0:T(8,128)(2,1)} %get-tuple-element.78), calls=%async_computation.5 | async-start | bytes 393216 | tf_op jit(solution)/shard_map/all_to_all | solution.py:401
  192.9 9.4 %copy-start.11 = (bf16[3584,4096]{1,0:T(8,128)(2,1)S(1)}, bf16[3584,4096]{1,0:T(8,128)(2,1)}, u32[]{:S(2)}) copy-start(bf16[3584,4096]{1,0:T(8,128)(2,1)} %copy-done.10) | copy-start | bytes 88080384
  206.8 9.7 %copy-start.12 = (bf16[3584,4096]{1,0:T(8,128)(2,1)}, bf16[3584,4096]{1,0:T(8,128)(2,1)S(1)}, u32[]{:S(2)}) copy-start(bf16[3584,4096]{1,0:T(8,128)(2,1)S(1)} %get-tuple-element.79.held_ref) | copy-start | bytes 88080384
  216.5 31.4 %all-to-all-start.4 = ((bf16[8,32,256]{2,1,0:T(8,128)(2,1)}), bf16[8,32,256]{2,1,0:T(8,128)(2,1)S(1)}, u32[]{:S(2)}, u32[]{:S(2)}) async-start(bf16[8,32,256]{2,1,0:T(8,128)(2,1)} %get-tuple-element.77.after_ref), calls=%async_computation.4 | async-start | bytes 262144 | tf_op jit(solution)/shard_map/all_to_all | solution.py:401
  222.5 9.4 %copy-start.13 = (bf16[3584,4096]{1,0:T(8,128)(2,1)S(1)}, bf16[3584,4096]{1,0:T(8,128)(2,1)}, u32[]{:S(2)}) copy-start(bf16[3584,4096]{1,0:T(8,128)(2,1)} %copy-done.12) | copy-start | bytes 88080384
  238.2 9.7 %copy-start.14 = (bf16[3584,4096]{1,0:T(8,128)(2,1)}, bf16[3584,4096]{1,0:T(8,128)(2,1)S(1)}, u32[]{:S(2)}) copy-start(bf16[3584,4096]{1,0:T(8,128)(2,1)S(1)} %get-tuple-element.80.held_ref) | copy-start | bytes 88080384
  247.9 26.8 %all-to-all-start.7 = ((bf16[8,32,256]{2,1,0:T(8,128)(2,1)}), bf16[8,32,256]{2,1,0:T(8,128)(2,1)S(1)}, u32[]{:S(2)}, u32[]{:S(2)}) async-start(bf16[8,32,256]{2,1,0:T(8,128)(2,1)} %get-tuple-element.83), calls=%async_computation.7 | async-start | bytes 262144 | tf_op jit(solution)/shard_map/all_to_all | solution.py:401
  253.9 9.4 %copy-start.15 = (bf16[3584,4096]{1,0:T(8,128)(2,1)S(1)}, bf16[3584,4096]{1,0:T(8,128)(2,1)}, u32[]{:S(2)}) copy-start(bf16[3584,4096]{1,0:T(8,128)(2,1)} %copy-done.14) | copy-start | bytes 88080384
  265.0 9.7 %copy-start.16 = (bf16[3584,4096]{1,0:T(8,128)(2,1)}, bf16[3584,4096]{1,0:T(8,128)(2,1)S(1)}, u32[]{:S(2)}) copy-start(bf16[3584,4096]{1,0:T(8,128)(2,1)S(1)} %get-tuple-element.84.refs_1_) | copy-start | bytes 88080384
  274.7 31.8 %all-to-all-start.6 = ((bf16[8,32,256]{2,1,0:T(8,128)(2,1)}), bf16[8,32,256]{2,1,0:T(8,128)(2,1)S(1)}, u32[]{:S(2)}, u32[]{:S(2)}) async-start(bf16[8,32,256]{2,1,0:T(8,128)(2,1)} %get-tuple-element.82), calls=%async_computation.6 | async-start | bytes 262144 | tf_op jit(solution)/shard_map/all_to_all | solution.py:401
  280.7 9.4 %copy-start.17 = (bf16[3584,4096]{1,0:T(8,128)(2,1)S(1)}, bf16[3584,4096]{1,0:T(8,128)(2,1)}, u32[]{:S(2)}) copy-start(bf16[3584,4096]{1,0:T(8,128)(2,1)} %copy-done.16) | copy-start | bytes 88080384
  296.8 9.7 %copy-start.18 = (bf16[3584,4096]{1,0:T(8,128)(2,1)}, bf16[3584,4096]{1,0:T(8,128)(2,1)S(1)}, u32[]{:S(2)}) copy-start(bf16[3584,4096]{1,0:T(8,128)(2,1)S(1)} %get-tuple-element.85.refs_1_) | copy-start | bytes 88080384
  307.2 9.4 %copy-start.19 = (bf16[3584,4096]{1,0:T(8,128)(2,1)S(1)}, bf16[3584,4096]{1,0:T(8,128)(2,1)}, u32[]{:S(2)}) copy-start(bf16[3584,4096]{1,0:T(8,128)(2,1)} %copy-done.18) | copy-start | bytes 88080384
  328.3 9.7 %copy-start.20 = (bf16[3584,4096]{1,0:T(8,128)(2,1)}, bf16[3584,4096]{1,0:T(8,128)(2,1)S(1)}, u32[]{:S(2)}) copy-start(bf16[3584,4096]{1,0:T(8,128)(2,1)S(1)} %get-tuple-element.89.d_ref) | copy-start | bytes 88080384
  338.0 29.6 %all-to-all-start.9 = ((bf16[8,32,384]{2,1,0:T(8,128)(2,1)}), bf16[8,32,384]{2,1,0:T(8,128)(2,1)S(1)}, u32[]{:S(2)}, u32[]{:S(2)}) async-start(bf16[8,32,384]{2,1,0:T(8,128)(2,1)} %get-tuple-element.91), calls=%async_computation.9 | async-start | bytes 393216 | tf_op jit(solution)/shard_map/all_to_all | solution.py:401
  357.9 9.7 %copy-start.22 = (bf16[3584,4096]{1,0:T(8,128)(2,1)}, bf16[3584,4096]{1,0:T(8,128)(2,1)S(1)}, u32[]{:S(2)}) copy-start(bf16[3584,4096]{1,0:T(8,128)(2,1)S(1)} %get-tuple-element.92.held_ref) | copy-start | bytes 88080384
  367.6 31.4 %all-to-all-start.8 = ((bf16[8,32,256]{2,1,0:T(8,128)(2,1)}), bf16[8,32,256]{2,1,0:T(8,128)(2,1)S(1)}, u32[]{:S(2)}, u32[]{:S(2)}) async-start(bf16[8,32,256]{2,1,0:T(8,128)(2,1)} %get-tuple-element.90.after_ref), calls=%async_computation.8 | async-start | bytes 262144 | tf_op jit(solution)/shard_map/all_to_all | solution.py:401
  373.6 9.4 %copy-start.23 = (bf16[3584,4096]{1,0:T(8,128)(2,1)S(1)}, bf16[3584,4096]{1,0:T(8,128)(2,1)}, u32[]{:S(2)}) copy-start(bf16[3584,4096]{1,0:T(8,128)(2,1)} %copy-done.22) | copy-start | bytes 88080384
  389.3 9.7 %copy-start.24 = (bf16[3584,4096]{1,0:T(8,128)(2,1)}, bf16[3584,4096]{1,0:T(8,128)(2,1)S(1)}, u32[]{:S(2)}) copy-start(bf16[3584,4096]{1,0:T(8,128)(2,1)S(1)} %get-tuple-element.93.held_ref) | copy-start | bytes 88080384
  399.0 26.8 %all-to-all-start.11 = ((bf16[8,32,256]{2,1,0:T(8,128)(2,1)}), bf16[8,32,256]{2,1,0:T(8,128)(2,1)S(1)}, u32[]{:S(2)}, u32[]{:S(2)}) async-start(bf16[8,32,256]{2,1,0:T(8,128)(2,1)} %get-tuple-element.96), calls=%async_computation.11 | async-start | bytes 262144 | tf_op jit(solution)/shard_map/all_to_all | solution.py:401
  405.0 9.4 %copy-start.25 = (bf16[3584,4096]{1,0:T(8,128)(2,1)S(1)}, bf16[3584,4096]{1,0:T(8,128)(2,1)}, u32[]{:S(2)}) copy-start(bf16[3584,4096]{1,0:T(8,128)(2,1)} %copy-done.24) | copy-start | bytes 88080384
  416.1 9.7 %copy-start.26 = (bf16[3584,4096]{1,0:T(8,128)(2,1)}, bf16[3584,4096]{1,0:T(8,128)(2,1)S(1)}, u32[]{:S(2)}) copy-start(bf16[3584,4096]{1,0:T(8,128)(2,1)S(1)} %get-tuple-element.97.refs_1_) | copy-start | bytes 88080384
  425.8 31.8 %all-to-all-start.10 = ((bf16[8,32,256]{2,1,0:T(8,128)(2,1)}), bf16[8,32,256]{2,1,0:T(8,128)(2,1)S(1)}, u32[]{:S(2)}, u32[]{:S(2)}) async-start(bf16[8,32,256]{2,1,0:T(8,128)(2,1)} %get-tuple-element.95), calls=%async_computation.10 | async-start | bytes 262144 | tf_op jit(solution)/shard_map/all_to_all | solution.py:401
  431.8 9.4 %copy-start.27 = (bf16[3584,4096]{1,0:T(8,128)(2,1)S(1)}, bf16[3584,4096]{1,0:T(8,128)(2,1)}, u32[]{:S(2)}) copy-start(bf16[3584,4096]{1,0:T(8,128)(2,1)} %copy-done.26) | copy-start | bytes 88080384
  447.9 9.7 %copy-start.28 = (bf16[3584,4096]{1,0:T(8,128)(2,1)}, bf16[3584,4096]{1,0:T(8,128)(2,1)S(1)}, u32[]{:S(2)}) copy-start(bf16[3584,4096]{1,0:T(8,128)(2,1)S(1)} %get-tuple-element.98.refs_1_) | copy-start | bytes 88080384
  479.4 9.7 %copy-start.30 = (bf16[3584,4096]{1,0:T(8,128)(2,1)}, bf16[3584,4096]{1,0:T(8,128)(2,1)S(1)}, u32[]{:S(2)}) copy-start(bf16[3584,4096]{1,0:T(8,128)(2,1)S(1)} %get-tuple-element.102.d_ref) | copy-start | bytes 88080384
  489.1 29.6 %all-to-all-start.13 = ((bf16[8,32,384]{2,1,0:T(8,128)(2,1)}), bf16[8,32,384]{2,1,0:T(8,128)(2,1)S(1)}, u32[]{:S(2)}, u32[]{:S(2)}) async-start(bf16[8,32,384]{2,1,0:T(8,128)(2,1)} %get-tuple-element.104), calls=%async_computation.13 | async-start | bytes 393216 | tf_op jit(solution)/shard_map/all_to_all | solution.py:401
  495.1 9.4 %copy-start.31 = (bf16[3584,4096]{1,0:T(8,128)(2,1)S(1)}, bf16[3584,4096]{1,0:T(8,128)(2,1)}, u32[]{:S(2)}) copy-start(bf16[3584,4096]{1,0:T(8,128)(2,1)} %copy-done.30) | copy-start | bytes 88080384
  509.0 9.7 %copy-start.32 = (bf16[3584,4096]{1,0:T(8,128)(2,1)}, bf16[3584,4096]{1,0:T(8,128)(2,1)S(1)}, u32[]{:S(2)}) copy-start(bf16[3584,4096]{1,0:T(8,128)(2,1)S(1)} %get-tuple-element.105.held_ref) | copy-start | bytes 88080384
  518.7 31.4 %all-to-all-start.12 = ((bf16[8,32,256]{2,1,0:T(8,128)(2,1)}), bf16[8,32,256]{2,1,0:T(8,128)(2,1)S(1)}, u32[]{:S(2)}, u32[]{:S(2)}) async-start(bf16[8,32,256]{2,1,0:T(8,128)(2,1)} %get-tuple-element.103.after_ref), calls=%async_computation.12 | async-start | bytes 262144 | tf_op jit(solution)/shard_map/all_to_all | solution.py:401
  524.7 9.4 %copy-start.33 = (bf16[3584,4096]{1,0:T(8,128)(2,1)S(1)}, bf16[3584,4096]{1,0:T(8,128)(2,1)}, u32[]{:S(2)}) copy-start(bf16[3584,4096]{1,0:T(8,128)(2,1)} %copy-done.32) | copy-start | bytes 88080384
  540.4 9.7 %copy-start.34 = (bf16[3584,4096]{1,0:T(8,128)(2,1)}, bf16[3584,4096]{1,0:T(8,128)(2,1)S(1)}, u32[]{:S(2)}) copy-start(bf16[3584,4096]{1,0:T(8,128)(2,1)S(1)} %get-tuple-element.106.held_ref) | copy-start | bytes 88080384
  550.1 26.8 %all-to-all-start.15 = ((bf16[8,32,256]{2,1,0:T(8,128)(2,1)}), bf16[8,32,256]{2,1,0:T(8,128)(2,1)S(1)}, u32[]{:S(2)}, u32[]{:S(2)}) async-start(bf16[8,32,256]{2,1,0:T(8,128)(2,1)} %get-tuple-element.109), calls=%async_computation.15 | async-start | bytes 262144 | tf_op jit(solution)/shard_map/all_to_all | solution.py:401
  556.1 9.4 %copy-start.35 = (bf16[3584,4096]{1,0:T(8,128)(2,1)S(1)}, bf16[3584,4096]{1,0:T(8,128)(2,1)}, u32[]{:S(2)}) copy-start(bf16[3584,4096]{1,0:T(8,128)(2,1)} %copy-done.34) | copy-start | bytes 88080384
  567.2 9.7 %copy-start.36 = (bf16[3584,4096]{1,0:T(8,128)(2,1)}, bf16[3584,4096]{1,0:T(8,128)(2,1)S(1)}, u32[]{:S(2)}) copy-start(bf16[3584,4096]{1,0:T(8,128)(2,1)S(1)} %get-tuple-element.110.refs_1_) | copy-start | bytes 88080384
  576.9 31.8 %all-to-all-start.14 = ((bf16[8,32,256]{2,1,0:T(8,128)(2,1)}), bf16[8,32,256]{2,1,0:T(8,128)(2,1)S(1)}, u32[]{:S(2)}, u32[]{:S(2)}) async-start(bf16[8,32,256]{2,1,0:T(8,128)(2,1)} %get-tuple-element.108), calls=%async_computation.14 | async-start | bytes 262144 | tf_op jit(solution)/shard_map/all_to_all | solution.py:401
  582.9 9.4 %copy-start.37 = (bf16[3584,4096]{1,0:T(8,128)(2,1)S(1)}, bf16[3584,4096]{1,0:T(8,128)(2,1)}, u32[]{:S(2)}) copy-start(bf16[3584,4096]{1,0:T(8,128)(2,1)} %copy-done.36) | copy-start | bytes 88080384
  599.0 9.7 %copy-start.38 = (bf16[3584,4096]{1,0:T(8,128)(2,1)}, bf16[3584,4096]{1,0:T(8,128)(2,1)S(1)}, u32[]{:S(2)}) copy-start(bf16[3584,4096]{1,0:T(8,128)(2,1)S(1)} %get-tuple-element.111.refs_1_) | copy-start | bytes 88080384
  609.4 9.4 %copy-start.39 = (bf16[3584,4096]{1,0:T(8,128)(2,1)S(1)}, bf16[3584,4096]{1,0:T(8,128)(2,1)}, u32[]{:S(2)}) copy-start(bf16[3584,4096]{1,0:T(8,128)(2,1)} %copy-done.38) | copy-start | bytes 88080384
  618.7 10.4 %copy-start.41 = (bf16[8,32,256]{2,1,0:T(8,128)(2,1)S(1)}, bf16[8,32,256]{2,1,0:T(8,128)(2,1)}, u32[]{:S(2)}) copy-start(bf16[8,32,256]{2,1,0:T(8,128)(2,1)} %copy-done.40) | copy-start | bytes 393220
  625.7 14.7 %all-to-all-start.16 = ((bf16[4,32,896]{2,1,0:T(8,128)(2,1)}), bf16[4,32,896]{2,1,0:T(8,128)(2,1)S(1)}, u32[]{:S(2)}, u32[]{:S(2)}) async-start(bf16[4,32,896]{2,1,0:T(8,128)(2,1)} %get-tuple-element.113), calls=%async_computation.16 | async-start | bytes 458752 | tf_op jit(solution)/shard_map/all_to_all | solution.py:401
  629.1 8.9 %collective-permute-start = (bf16[8,32,256]{2,1,0:T(8,128)(2,1)S(1)}, bf16[8,32,256]{2,1,0:T(8,128)(2,1)S(1)}, u32[]{:S(2)}, u32[]{:S(2)}) collective-permute-start(bf16[8,32,256]{2,1,0:T(8,128)(2,1)S(1)} %copy-done.41), channel_id=1, source_target_pairs={{0,16},{8,24},{16,0},{24,8},{1,17},{9,25},{17,1},{25,9},{2,18},{10... | collective-permute-start | bytes 393224 | tf_op jit(solution)/shard_map/ppermute | solution.py:409
  631.1 9.3 %collective-permute-start.3 = (bf16[8,32,256]{2,1,0:T(8,128)(2,1)}, bf16[8,32,256]{2,1,0:T(8,128)(2,1)S(1)}, u32[]{:S(2)}, u32[]{:S(2)}) collective-permute-start(bf16[8,32,256]{2,1,0:T(8,128)(2,1)} %copy-done.42), channel_id=1, source_target_pairs={{0,16},{8,24},{16,0},{24,8},{1,17},{9,25},{17,1},{25,9},{2,18},{10... | collective-permute-start | bytes 393224 | tf_op jit(solution)/shard_map/ppermute | solution.py:409
  631.2 26.3 %collective-permute-start.1 = (bf16[8,32,256]{2,1,0:T(8,128)(2,1)S(1)}, bf16[8,32,256]{2,1,0:T(8,128)(2,1)S(1)}, u32[]{:S(2)}, u32[]{:S(2)}) collective-permute-start(bf16[8,32,256]{2,1,0:T(8,128)(2,1)S(1)} %copy-done.41), channel_id=1, source_target_pairs={{0,8},{8,0},{16,24},{24,16},{1,9},{9,1},{17,25},{25,17},{2,10},{10... | collective-permute-start | bytes 393224 | tf_op jit(solution)/shard_map/ppermute | solution.py:409
  631.2 26.3 %collective-permute-start.4 = (bf16[8,32,256]{2,1,0:T(8,128)(2,1)}, bf16[8,32,256]{2,1,0:T(8,128)(2,1)S(1)}, u32[]{:S(2)}, u32[]{:S(2)}) collective-permute-start(bf16[8,32,256]{2,1,0:T(8,128)(2,1)} %copy-done.42), channel_id=1, source_target_pairs={{0,8},{8,0},{16,24},{24,16},{1,9},{9,1},{17,25},{25,17},{2,10},{10... | collective-permute-start | bytes 393224 | tf_op jit(solution)/shard_map/ppermute | solution.py:409
  638.0 19.5 %collective-permute-start.2 = (bf16[8,32,256]{2,1,0:T(8,128)(2,1)S(1)}, bf16[8,32,256]{2,1,0:T(8,128)(2,1)S(1)}, u32[]{:S(2)}, u32[]{:S(2)}) collective-permute-start(bf16[8,32,256]{2,1,0:T(8,128)(2,1)S(1)} %collective-permute-done.refs_1_), channel_id=1, source_target_pairs={{0,8},{8,0},{16,24},{24,16},{1,9},{9,1},{17,25},{25,17},{2,10},{10... | collective-permute-start | bytes 393224 | tf_op jit(solution)/shard_map/ppermute | solution.py:409
  640.3 17.1 %collective-permute-start.5 = (bf16[8,32,256]{2,1,0:T(8,128)(2,1)S(1)}, bf16[8,32,256]{2,1,0:T(8,128)(2,1)S(1)}, u32[]{:S(2)}, u32[]{:S(2)}) collective-permute-start(bf16[8,32,256]{2,1,0:T(8,128)(2,1)S(1)} %collective-permute-done.3.refs_5_), channel_id=1, source_target_pairs={{0,8},{8,0},{16,24},{24,16},{1,9},{9,1},{17,25},{25,17},{2,10},{10... | collective-permute-start | bytes 393224 | tf_op jit(solution)/shard_map/ppermute | solution.py:409
  641.2 12.9 %all-to-all-start.17 = ((f32[8,16,128]{2,1,0:T(8,128)}), f32[8,16,128]{2,1,0:T(8,128)S(1)}, u32[]{:S(2)}, u32[]{:S(2)}) async-start(f32[8,16,128]{2,1,0:T(8,128)} %left_partial.1), calls=%async_computation.17 | async-start | bytes 131072 | tf_op jit(solution)/shard_map/all_to_all | solution.py:401
  654.8 15.7 %all-to-all-start.18 = ((f32[32,16,128]{2,1,0:T(8,128)}), f32[32,16,128]{2,1,0:T(8,128)S(1)}, u32[]{:S(2)}, u32[]{:S(2)}) async-start(f32[32,16,128]{2,1,0:T(8,128)} %broadcast_in_dim.2), calls=%async_computation.18 | async-start | bytes 524288 | tf_op jit(solution)/shard_map/all_to_all | solution.py:401
  (19 other events, 94.2 us)

commit v3 on v0

v3 whole, which is shorter than its diff:
```python
import functools

import jax
import jax.numpy as jnp
from jax import lax
from jax.experimental import pallas as pl
from jax.experimental.pallas import tpu as pltpu
from jax.sharding import PartitionSpec as P

ITERS = 4
ROOT_STEPS = 12
LANES = 128
TILE = 8
F32 = jnp.float32
BF16 = jnp.bfloat16
ROWS_BY_ROWS = (((1,), (1,)), ((), ()))
VMEM_BYTES = 16 * 1024 * 1024
IN_VMEM = pl.BlockSpec(memory_space=pltpu.VMEM)
ANYWHERE = pl.BlockSpec(memory_space=pl.ANY)


def shape_of(shape, kind):
    return jax.ShapeDtypeStruct(shape, kind)


def call(kernel, name, operands, shapes, scratch=(), held=None, idle=(), flops=10**8):
    operands = [*operands, *idle]
    specs = [IN_VMEM] * (len(operands) - len(idle)) + [ANYWHERE] * len(idle)
    if held is not None:
        operands, specs = [held, *operands], [IN_VMEM, *specs]
    return pl.pallas_call(
        kernel,
        out_shape=tuple(shapes),
        in_specs=specs,
        out_specs=(IN_VMEM,) * len(shapes),
        scratch_shapes=list(scratch),
        cost_estimate=pl.CostEstimate(flops=flops, bytes_accessed=10**6, transcendentals=0),
        compiler_params=pltpu.CompilerParams(vmem_limit_bytes=VMEM_BYTES),
        name=name,
    )(*operands)


def split_two(value):
    high = value.astype(BF16)
    return high, (value - high.astype(F32)).astype(BF16)


def split_three(value):
    high = value.astype(BF16)
    rest = value - high.astype(F32)
    middle = rest.astype(BF16)
    return high, middle, (rest - middle.astype(F32)).astype(BF16)


def spread(value, order, axis):
    pieces = split_three(value)
    return jnp.concatenate([pieces[at] for at in order], axis=axis)


def square(left, right):
    return jnp.dot(
        spread(left, (0, 0, 1, 0, 2, 1), 1), spread(right, (0, 1, 0, 2, 0, 1), 0), preferred_element_type=F32
    )


def eye_of(size):
    return lax.broadcasted_iota(jnp.int32, (size, size), 0) == lax.broadcasted_iota(jnp.int32, (size, size), 1)


def tree_sum(values):
    while len(values) > 1:
        values = [values[at] + values[at + 1] for at in range(0, len(values), 2)]
    return values[0]


def lower_inverse(grams):
    size = grams[0].shape[0]
    tiles = size // TILE
    rows = lax.broadcasted_iota(jnp.int32, (TILE, LANES), 0)
    lanes = lax.broadcasted_iota(jnp.int32, (TILE, LANES), 1)
    columns, inverses, scales = [], [], []
    for gram in grams:
        wide = [jnp.broadcast_to(gram[:, at : at + 1], (size, LANES)) for at in range(size)]
        columns.append([[one[TILE * tile : TILE * (tile + 1)] for tile in range(tiles)] for one in wide])
        inverses.append([(rows + TILE * tile == lanes).astype(F32) for tile in range(tiles)])
        scales.append([jnp.zeros((TILE, LANES), F32) for _ in range(tiles)])
    for step in range(size):
        top, place = divmod(step, TILE)
        for cols, inverse, scale in zip(columns, inverses, scales):
            pivot = cols[step][top][place : place + 1]
            reciprocal = 1.0 / pivot
            ratio = [None] * top + [cols[step][tile] * reciprocal for tile in range(top, tiles)]
            for later in range(step + 1, size):
                first, inner = divmod(later, TILE)
                factor = ratio[first][inner : inner + 1]
                for tile in range(first, tiles):
                    cols[later][tile] = cols[later][tile] - cols[step][tile] * factor
            own = inverse[top][place : place + 1]
            for tile in range(top, tiles):
                factor = jnp.where(rows > place, ratio[tile], 0.0) if tile == top else ratio[tile]
                inverse[tile] = inverse[tile] - factor * own
            scale[top] = jnp.where(rows == place, lax.rsqrt(pivot), scale[top])
    return [
        jnp.concatenate([one * down for one, down in zip(inverse, scale)], axis=0)[:, :size]
        for inverse, scale in zip(inverses, scales)
    ]


def gram_pieces(images):
    rank = images.shape[0]
    gram = lax.dot_general(images, images, ROWS_BY_ROWS, preferred_element_type=F32)
    return jnp.concatenate([*split_three(gram), jnp.zeros((rank, LANES - 3 * rank), BF16)], axis=1)


def tall_of(rows, *sizes):
    return next(size for size in (*sizes, rows) if rows % size == 0)


def partner(axis, mask):
    return lax.bitwise_xor(lax.axis_index(axis).astype(jnp.int32), jnp.int32(mask))


def block_at(index, size):
    return pl.ds(pl.multiple_of(index * size, size), size)


def first_kernel(tall, d_ref, x_ref, out_ref, gram_ref, wide):
    wide[...] = x_ref[...].astype(BF16)

    def body(at, carry):
        span = block_at(at, tall)
        product = lax.dot_general(wide[...], d_ref[span, :], ROWS_BY_ROWS, preferred_element_type=F32)
        out_ref[:, span] = product.astype(BF16)
        return carry

    lax.fori_loop(0, d_ref.shape[0] // tall, body, 0)
    gram_ref[...] = gram_pieces(out_ref[...])


def first(held, start):
    rows, cols = held.shape
    rank = start.shape[0]
    return call(
        functools.partial(first_kernel, tall_of(rows, 512, 896, 256, 128)),
        "first",
        [start],
        [shape_of((rank, rows), BF16), shape_of((rank, LANES), BF16)],
        [pltpu.VMEM((rank, cols), BF16)],
        held=held,
        flops=2 * rows * cols * 384,
    )


def backs_kernel(masks, d_ref, images_ref, gram_ref, *out_refs):
    for mask, out_ref in zip(masks, out_refs[-len(masks) :]):
        chunk = out_ref.shape[1] - LANES
        span = block_at(partner("row", mask), chunk)
        out_ref[:, :LANES] = gram_ref[...]
        out_ref[:, LANES:] = jnp.dot(images_ref[...], d_ref[:, span], preferred_element_type=F32).astype(BF16)


def backs(held, panel, gram, masks, parts, *after):
    rows, cols = held.shape
    rank = panel.shape[0]
    pieces = call(
        functools.partial(backs_kernel, masks),
        "backs",
        [panel, gram],
        [shape_of((rank, cols // parts + LANES), BF16)] * len(masks),
        held=held,
        idle=after,
        flops=2 * rows * cols * 256 // parts * len(masks),
    )
    return dict(zip(masks, pieces))


def settle_kernel(_, *refs):
    *in_refs, out_ref = refs
    total = tree_sum([ref[...].astype(F32) for ref in in_refs])
    rank = total.shape[0]
    gram = total[:, :rank] + total[:, rank : 2 * rank] + total[:, 2 * rank : 3 * rank]
    out_ref[...] = square(lower_inverse([gram])[0], total[:, LANES:]).astype(BF16)


def settle(held, pieces):
    rank, wide = pieces[0].shape
    return call(settle_kernel, "settle", pieces, [shape_of((rank, wide - LANES), BF16)], held=held)


def images_kernel(masks, tall, partial, tasks, d_ref, *refs):
    x_refs, refs = refs[: len(masks)], refs[len(masks) :]
    if partial:
        sum_ref, refs = refs[0], refs[1:]
    target = refs[-2] if tasks else refs[0]
    chunk = x_refs[0].shape[1]

    def body(at, carry):
        span = block_at(at, tall)
        product = sum_ref[:, span] if partial else None
        for mask, x_ref in zip(masks, x_refs):
            term = lax.dot_general(
                x_ref[...],
                d_ref[span, block_at(partner("row", mask), chunk)],
                ROWS_BY_ROWS,
                preferred_element_type=F32,
            )
            product = term if product is None else product + term
        target[:, span] = product.astype(target.dtype)
        return carry

    lax.fori_loop(0, d_ref.shape[0] // tall, body, 0)
    if tasks:
        *out_refs, flat, stacked = refs
        each = stacked.shape[2]
        for at in range(tasks):
            stacked[at] = flat[:, at * each : (at + 1) * each]
        for mask, out_ref in enumerate(out_refs):
            out_ref[...] = stacked[partner("task", mask)]
    elif len(refs) == 2:
        refs[1][...] = gram_pieces(refs[0][...])


def images(held, blocks, masks, partial=None, last=False, tasks=0):
    rows, cols = held.shape
    rank = blocks[0].shape[0]
    scratch = ()
    if tasks:
        shapes = [shape_of((rank, rows // tasks), BF16)] * tasks
        scratch = [pltpu.VMEM((rank, rows), BF16), pltpu.VMEM((tasks, rank, rows // tasks), BF16)]
    elif last:
        shapes = [shape_of((rank, rows), BF16), shape_of((rank, LANES), BF16)]
    else:
        shapes = [shape_of((rank, rows), F32)]
    return call(
        functools.partial(images_kernel, masks, tall_of(rows, 512, 896, 256, 128), partial is not None, tasks),
        "images",
        [blocks[mask] for mask in masks] + ([] if partial is None else [partial]),
        shapes,
        scratch,
        held=held,
        flops=2 * rows * cols * 384 * len(masks) // len(blocks),
    )


def pack_kernel(_, *refs):
    *in_refs, out_ref = refs
    chunk = in_refs[0].shape[1]
    for mask, in_ref in enumerate(in_refs):
        out_ref[:, block_at(partner("row", mask), chunk)] = in_ref[...]


def left_kernel(*refs):
    tasks = next(at for at, ref in enumerate(refs) if ref.shape != refs[0].shape)
    in_refs, panel_ref, out_refs, gram = refs[:tasks], refs[tasks], refs[tasks + 1 : -1], refs[-1]
    rank = in_refs[0].shape[0]
    for mask, in_ref in enumerate(in_refs):
        panel_ref[block_at(partner("task", mask), rank), :] = in_ref[...]
    gram[...] = lax.dot_general(panel_ref[...], panel_ref[...], ROWS_BY_ROWS, preferred_element_type=F32)
    for mask, out_ref in enumerate(out_refs):
        out_ref[...] = gram[block_at(partner("row", mask), out_ref.shape[0]), :]


def left(pieces, parts):
    tasks = len(pieces)
    rank, each = pieces[0].shape
    size = tasks * rank
    return call(
        left_kernel,
        "left",
        pieces,
        [shape_of((size, each), BF16)] + [shape_of((size // parts, size), F32)] * parts,
        [pltpu.VMEM((size, size), F32)],
    )


def total_kernel(count, *refs):
    refs[-1][...] = tree_sum([ref[...] for ref in refs[:count]])


def total(pieces, after):
    return call(
        functools.partial(total_kernel, len(pieces)),
        "total",
        pieces,
        [shape_of(pieces[0].shape, F32)],
        idle=[after],
        flops=10**6,
    )[0]


def root_begin(gram):
    return gram / jnp.sqrt(jnp.sum(gram * gram)), eye_of(gram.shape[0]).astype(F32)


def root_steps(state, count):
    identity = eye_of(state[0].shape[0]).astype(F32)

    def step(_, state):
        upper, lower = state
        middle = 0.5 * (3.0 * identity - square(lower, upper))
        return square(upper, middle), square(middle, lower)

    return lax.fori_loop(0, count, step, state)


def root_end(state, gram):
    return state[1] / jnp.sqrt(jnp.sqrt(jnp.sum(gram * gram)))


def right_first_kernel(*refs):
    in_refs, (wide_ref, lower_ref, gram_ref) = refs[:-3], refs[-3:]
    rank = in_refs[0].shape[0]
    for mask, in_ref in enumerate(in_refs):
        wide_ref[block_at(partner("task", mask), rank), :] = in_ref[...]
    wide = wide_ref[...]
    raw = lax.dot_general(wide, wide, ROWS_BY_ROWS, preferred_element_type=F32)
    spans = [slice(task * rank, (task + 1) * rank) for task in range(len(in_refs))]
    lower_ref[...] = jnp.zeros_like(lower_ref)
    for span, inverse in zip(spans, lower_inverse([raw[span, span] for span in spans])):
        lower_ref[span, span] = inverse
    lower = lower_ref[...]
    gram_ref[...] = square(square(lower, raw), lower.T)


def right_second_kernel(gram_ref, upper_ref, lower_ref):
    upper_ref[...], lower_ref[...] = root_steps(root_begin(gram_ref[...]), ROOT_STEPS // 2)


def right_third_kernel(gram_ref, upper_ref, lower_ref, change_ref, out_ref):
    state = root_steps((upper_ref[...], lower_ref[...]), ROOT_STEPS - ROOT_STEPS // 2)
    out_ref[...] = square(root_end(state, gram_ref[...]).T, change_ref[...])


def finish_kernel(parts, *refs):
    gram_refs, (panel_ref, wide_ref, lower_ref, right_ref, out_ref, raw, side) = refs[:parts], refs[parts:]
    size = lower_ref.shape[0]

    @pl.when(pl.program_id(0) == 0)
    def _():
        for mask, gram_ref in enumerate(gram_refs):
            raw[block_at(partner("row", mask), gram_ref.shape[0]), :] = gram_ref[...]
        lower = lower_ref[...]
        gram = square(square(lower, raw[...]), lower.T)
        diagonal = jnp.where(eye_of(size), gram, 0.0)
        down = jnp.sqrt(jnp.sum(diagonal, axis=1, keepdims=True))
        across = jnp.sqrt(jnp.sum(diagonal, axis=0, keepdims=True))
        normed = gram / (down * across)
        mixing = root_end(root_steps(root_begin(normed), ROOT_STEPS), normed) / down * across
        mixed = square(square(lower.T, mixing), right_ref[...])
        panel = panel_ref[...].T
        product = jnp.dot(
            jnp.concatenate([panel, panel], axis=1),
            jnp.concatenate(split_two(mixed), axis=0),
            preferred_element_type=F32,
        )
        side[...] = jnp.concatenate(split_two(product), axis=1)

    wide = wide_ref[...]
    out_ref[...] = jnp.dot(
        side[...], jnp.concatenate([wide, wide], axis=0), preferred_element_type=F32
    ).astype(BF16)


def finish(grams, panel, wide, lower, right_side):
    size, rows = panel.shape
    cols = wide.shape[1]
    across = 512

    def whole(array):
        return pl.BlockSpec(array.shape, lambda at: (0, 0))

    return pl.pallas_call(
        functools.partial(finish_kernel, len(grams)),
        out_shape=shape_of((rows, cols), BF16),
        grid=(cols // across,),
        in_specs=[
            *map(whole, grams),
            whole(panel),
            pl.BlockSpec((size, across), lambda at: (0, at)),
            whole(lower),
            whole(right_side),
        ],
        out_specs=pl.BlockSpec((rows, across), lambda at: (0, at)),
        scratch_shapes=[pltpu.VMEM((size, size), F32), pltpu.VMEM((rows, 2 * size), BF16)],
        compiler_params=pltpu.CompilerParams(vmem_limit_bytes=VMEM_BYTES),
        name="finish",
    )(*grams, panel, wide, lower, right_side)


def send(piece, axis, mask, count):
    return lax.ppermute(piece, axis, [(at, at ^ mask) for at in range(count)]) if mask else piece


def swap(pieces, axis):
    return [send(pieces[mask], axis, mask, len(pieces)) for mask in range(len(pieces))]


def share(piece, axis, count):
    return [send(piece, axis, mask, count) for mask in range(count)]


def spread_over_tasks(block, tasks):
    masks, blocks = [0], [block]
    bit = tasks // 2
    while bit:
        blocks = blocks + [send(each, "task", bit, tasks) for each in blocks]
        masks = masks + [mask ^ bit for mask in masks]
        bit //= 2
    return [block for _, block in sorted(zip(masks, blocks), key=lambda pair: pair[0])]


def local(tasks, parts, task_delta, start_block):
    near, far = tuple(range(1, parts // 2)), tuple(range(parts // 2, parts))
    size = tasks * start_block.shape[2]
    held = pltpu.with_memory_space_constraint(task_delta[0], pltpu.VMEM)
    panel, gram = first(held, start_block[0].T)
    for step in range(ITERS):
        last = step == ITERS - 1
        away = backs(held, panel, gram, far, parts)
        close = backs(held, panel, gram, (*near, 0), parts, away[far[0]])
        (block,) = settle(held, swap({**away, **close}, "row"))
        blocks = share(block, "row", parts)
        (partial,) = images(held, blocks, (0,))
        (partial,) = images(held, blocks, near, partial)
        if last:
            (own,) = call(
                pack_kernel, "pack", blocks, [shape_of((block.shape[0], held.shape[1]), BF16)], held=held
            )
            pieces = images(held, blocks, far, partial, tasks=tasks)
        else:
            panel, gram = images(held, blocks, far, partial, last=True)
    panel, *grams = left(swap(pieces, "task"), parts)
    square_shape = shape_of((size, size), F32)
    wide, lower, right_gram = call(
        right_first_kernel,
        "right_first",
        spread_over_tasks(own, tasks),
        [shape_of((size, held.shape[1]), BF16), square_shape, square_shape],
    )
    part = total(swap(grams, "row"), lower)
    state = call(right_second_kernel, "right_second", [right_gram], [square_shape] * 2)
    part = total(share(part, "task", tasks), state[0])
    right_side = call(right_third_kernel, "right_third", [right_gram, *state, lower], [square_shape])[0]
    return finish(share(part, "row", parts), panel, wide, lower, right_side)


def solution(mesh):
    tasks, parts = mesh.shape["task"], mesh.shape["row"]
    placed = (P("task", "row", None), P("task", None, None))
    return jax.shard_map(
        functools.partial(local, tasks, parts),
        mesh=mesh,
        in_specs=placed,
        out_specs=P(("row", "task"), None),
        check_vma=False,
    )
```

time: 668 us -> 252 us (0.38); the launches traced: 661 us -> 252 us
  waiting for transfers between devices: 417 us -> 25.8 us
  matrix products: 188 us -> 0 us
  starting transfers between devices: 0.6 us -> 114 us
  Pallas kernels: 0 us -> 101 us
  other arithmetic: 28.4 us -> 0 us
  between operations: 16.1 us -> 0.44 us
  blocking collectives: 8.22 us -> 0 us
  local copies, waits for them, and re-layouts: 2.26 us -> 10.4 us
    psum x5 -> x0, waiting for transfers between devices: 406 us -> none  [the longest x4 290 us: local(): backs = lax.psum(partial_value, 'row')]
    dot_general x84 -> x0, matrix products: 182 us -> none  [the longest x4 120 us: local(): lax.dot_general(local_rows, images, (((0,), (0,)), ((), ())), preferred_e...]
    ppermute x0 -> x79, starting transfers between devices: none -> 114 us  [send(): lax.ppermute(piece, axis, [(at, at ^ mask) for at in range(count)])]
    pallas_call x0 -> x33, Pallas kernels: none -> 101 us  [the longest x32 88.8 us: call(): pl.pallas_call(kernel, out_shape=tuple(shapes), in_specs=specs, out_specs...]
    another operation x21 -> x0, other arithmetic: 26.7 us -> none  [the longest x12 14.4 us: orthonormal(): factor = jnp.linalg.cholesky(gram)]
    ppermute x0 -> x79, waiting for transfers between devices: none -> 25.8 us  [send(): lax.ppermute(piece, axis, [(at, at ^ mask) for at in range(count)])]
    all_gather x1 -> x0, waiting for transfers between devices: 11.2 us -> none  [local(): bases = lax.all_gather(current, 'task', axis=1, tiled=True)]
    unnamed x2 -> x4, local copies, waits for them, and re-layouts: 0.01 us -> 10.4 us
  transfers between devices with their start and end apart: 6 -> 79, of which waited for: 6 -> 22; matrix products, arithmetic and copies ran while one was open for 2% -> 0% of each run, Pallas kernels for 0% -> 19%
where the time goes in v3:
time: 252 us
  starting transfers between devices  114 us (45%)
  Pallas kernels  101 us (40%)
  waiting for transfers between devices  25.8 us (10%)
  local copies, waits for them, and re-layouts  10.4 us (4%)
    ppermute x79, starting transfers between devices, send(): lax.ppermute(piece, axis, [(at, at ^ mask) for at in range(count)])  114 us
    pallas_call x32, Pallas kernels, call(): pl.pallas_call(kernel, out_shape=tuple(shapes), in_specs=specs, out_specs...  88.8 us
    ppermute x79, waiting for transfers between devices, send(): lax.ppermute(piece, axis, [(at, at ^ mask) for at in range(count)])  25.8 us
    pallas_call x1, Pallas kernels, finish(): pl.pallas_call(functools.partial(finish_kernel, len(grams)), out_shape=sh...  12.6 us
    unnamed x4, local copies, waits for them, and re-layouts  10.4 us
  transfers between devices with their start and end apart: 79, of which 22 were waited for; matrix products, arithmetic and copies ran while one was open for 0% of the time, Pallas kernels for 19%

profile of v3, /device:TPU:0, one launch (start us, length us, event | category | flops | bytes accessed | tf_op | source)
XLA Modules:
  0.0 252.0 jit_solution(8060744747849280773)
XLA Ops:
  0.0 9.3 %copy-done = bf16[1,3584,4096]{2,1,0:T(8,128)(2,1)S(1)} copy-done((bf16[1,3584,4096]{2,1,0:T(8,128)(2,1)S(1)}, bf16[1,3584,4096]{2,1,0:T(8,128)(2,1)}, u32[]{:S(2)}) %copy-start) | copy-done | bytes 29360152
  10.4 9.7 %first.1 = (bf16[32,3584]{1,0:T(8,128)(2,1)S(1)}, bf16[32,128]{1,0:T(8,128)(2,1)S(1)}) custom-call(bf16[3584,4096]{1,0:T(8,128)(2,1)S(1)} %bitcast.4, f32[32,4096]{1,0:T(8,128)S(1)} %bitcast.30), custom_call_target="tpu_custom_call" | custom-call | flops 11274289152 | bytes 1000000 | tf_op jit(solution)/shard_map/first/pallas_call | solution.py:31
  20.1 2.6 %backs.8 = (bf16[32,640]{1,0:T(8,128)(2,1)S(1)}, bf16[32,640]{1,0:T(8,128)(2,1)S(1)}, bf16[32,640]{1,0:T(8,128)(2,1)S(1)}, bf16[32,640]{1,0:T(8,128)(2,1)S(1)}) custom-call(bf16[3584,4096]{1,0:T(8,128)(2,1)S(1)} %bitcast.5, bf16[32,3584]{1,0:T(8,128)(2,1)S(1)} %get-tuple-element.63.images_ref, bf16[32,128]{1,0:T(8,128)(2,1)S(1)} %get-tuple-element.64.gram_ref), custom_call_target="tpu_custom_call" | custom-call | flops 3758096384 | bytes 1000000 | tf_op jit(solution)/shard_map/backs/pallas_call | solution.py:31
  22.8 5.0 %collective-permute-start.4 = (bf16[32,640]{1,0:T(8,128)(2,1)S(1)}, bf16[32,640]{1,0:T(8,128)(2,1)S(1)}, u32[]{:S(2)}, u32[]{:S(2)}) collective-permute-start(bf16[32,640]{1,0:T(8,128)(2,1)S(1)} %get-tuple-element.70), channel_id=1, source_target_pairs={{0,5},{1,4},{2,7},{3,6},{4,1},{5,0},{6,3},{7,2},{8,13},{9,12},{10,... | collective-permute-start | bytes 122888 | tf_op jit(solution)/shard_map/ppermute | solution.py:391
  29.1 2.4 collective-permute-start.6
  31.5 2.6 %backs.9 = (bf16[32,640]{1,0:T(8,128)(2,1)S(1)}, bf16[32,640]{1,0:T(8,128)(2,1)S(1)}, bf16[32,640]{1,0:T(8,128)(2,1)S(1)}, bf16[32,640]{1,0:T(8,128)(2,1)S(1)}) custom-call(bf16[3584,4096]{1,0:T(8,128)(2,1)S(1)} %bitcast.6, bf16[32,3584]{1,0:T(8,128)(2,1)S(1)} %get-tuple-element.63.images_ref, bf16[32,128]{1,0:T(8,128)(2,1)S(1)} %get-tuple-element.64.gram_ref, ...), custom_call_target="tpu_custom_call" | custom-call | flops 3758096384 | bytes 1000000 | tf_op jit(solution)/shard_map/backs/pallas_call | solution.py:31
  35.7 2.0 collective-permute-start.2
  44.5 2.0 collective-permute-start.12
  47.0 2.7 %collective-permute-start.10 = (bf16[32,512]{1,0:T(8,128)(2,1)S(1)}, bf16[32,512]{1,0:T(8,128)(2,1)S(1)}, u32[]{:S(2)}, u32[]{:S(2)}) collective-permute-start(bf16[32,512]{1,0:T(8,128)(2,1)S(1)} %settle.4.refs_0_), channel_id=1, source_target_pairs={{0,7},{1,6},{2,5},{3,4},{4,3},{5,2},{6,1},{7,0},{8,15},{9,14},{10,... | collective-permute-start | bytes 98312 | tf_op jit(solution)/shard_map/ppermute | solution.py:391
  49.8 2.1 collective-permute-start.9
  51.8 1.9 images.12.refs_3_
  53.8 2.9 %collective-permute-start.7 = (bf16[32,512]{1,0:T(8,128)(2,1)S(1)}, bf16[32,512]{1,0:T(8,128)(2,1)S(1)}, u32[]{:S(2)}, u32[]{:S(2)}) collective-permute-start(bf16[32,512]{1,0:T(8,128)(2,1)S(1)} %settle.4.refs_0_), channel_id=1, source_target_pairs={{0,4},{1,5},{2,6},{3,7},{4,0},{5,1},{6,2},{7,3},{8,12},{9,13},{10,... | collective-permute-start | bytes 98312 | tf_op jit(solution)/shard_map/ppermute | solution.py:391
  56.6 4.0 %images.13.refs_4_ = f32[32,3584]{1,0:T(8,128)S(1)} custom-call(bf16[3584,4096]{1,0:T(8,128)(2,1)S(1)} %bitcast.9, bf16[32,512]{1,0:T(8,128)(2,1)S(1)} %collective-permute-done.11.refs_0_, bf16[32,512]{1,0:T(8,128)(2,1)S(1)} %collective-permute-done.12.refs_1_, bf16[32,512]{1,0:T(8,128)(2,1)S(1)} %collective-permute-done.13.refs_2_, ...), custom_call_target="tpu_custom_call" | custom-call | flops 4227858432 | bytes 1000000 | tf_op jit(solution)/shard_map/images/pallas_call | solution.py:31
  60.7 5.4 %images.14 = (bf16[32,3584]{1,0:T(8,128)(2,1)S(1)}, bf16[32,128]{1,0:T(8,128)(2,1)S(1)}) custom-call(bf16[3584,4096]{1,0:T(8,128)(2,1)S(1)} %bitcast.10, bf16[32,512]{1,0:T(8,128)(2,1)S(1)} %collective-permute-done.7.refs_0_, bf16[32,512]{1,0:T(8,128)(2,1)S(1)} %collective-permute-done.8.refs_1_, bf16[32,512]{1,0:T(8,128)(2,1)S(1)} %collective-permute-done.9.refs_2_, ...), custom_call_target="tpu_custom_call" | custom-call | flops 5637144576 | bytes 1000000 | tf_op jit(solution)/shard_map/images/pallas_call | solution.py:31
  66.1 2.6 %backs.10 = (bf16[32,640]{1,0:T(8,128)(2,1)S(1)}, bf16[32,640]{1,0:T(8,128)(2,1)S(1)}, bf16[32,640]{1,0:T(8,128)(2,1)S(1)}, bf16[32,640]{1,0:T(8,128)(2,1)S(1)}) custom-call(bf16[3584,4096]{1,0:T(8,128)(2,1)S(1)} %bitcast.11, bf16[32,3584]{1,0:T(8,128)(2,1)S(1)} %get-tuple-element.73.images_ref, bf16[32,128]{1,0:T(8,128)(2,1)S(1)} %get-tuple-element.74.gram_ref), custom_call_target="tpu_custom_call" | custom-call | flops 3758096384 | bytes 1000000 | tf_op jit(solution)/shard_map/backs/pallas_call | solution.py:31
  72.2 2.6 %backs.11 = (bf16[32,640]{1,0:T(8,128)(2,1)S(1)}, bf16[32,640]{1,0:T(8,128)(2,1)S(1)}, bf16[32,640]{1,0:T(8,128)(2,1)S(1)}, bf16[32,640]{1,0:T(8,128)(2,1)S(1)}) custom-call(bf16[3584,4096]{1,0:T(8,128)(2,1)S(1)} %bitcast.12, bf16[32,3584]{1,0:T(8,128)(2,1)S(1)} %get-tuple-element.73.images_ref, bf16[32,128]{1,0:T(8,128)(2,1)S(1)} %get-tuple-element.74.gram_ref, ...), custom_call_target="tpu_custom_call" | custom-call | flops 3758096384 | bytes 1000000 | tf_op jit(solution)/shard_map/backs/pallas_call | solution.py:31
  74.8 2.0 collective-permute-start.20
  78.3 2.0 collective-permute-start.16
  83.4 2.3 collective-permute-done.17.refs_4_
  87.2 2.2 collective-permute-start.26
  90.2 2.6 %collective-permute-start.24 = (bf16[32,512]{1,0:T(8,128)(2,1)S(1)}, bf16[32,512]{1,0:T(8,128)(2,1)S(1)}, u32[]{:S(2)}, u32[]{:S(2)}) collective-permute-start(bf16[32,512]{1,0:T(8,128)(2,1)S(1)} %settle.5.refs_0_), channel_id=1, source_target_pairs={{0,7},{1,6},{2,5},{3,4},{4,3},{5,2},{6,1},{7,0},{8,15},{9,14},{10,... | collective-permute-start | bytes 98312 | tf_op jit(solution)/shard_map/ppermute | solution.py:391
  92.8 1.9 collective-permute-start.23
  94.7 1.9 images.15.refs_3_
  96.7 3.1 %collective-permute-start.21 = (bf16[32,512]{1,0:T(8,128)(2,1)S(1)}, bf16[32,512]{1,0:T(8,128)(2,1)S(1)}, u32[]{:S(2)}, u32[]{:S(2)}) collective-permute-start(bf16[32,512]{1,0:T(8,128)(2,1)S(1)} %settle.5.refs_0_), channel_id=1, source_target_pairs={{0,4},{1,5},{2,6},{3,7},{4,0},{5,1},{6,2},{7,3},{8,12},{9,13},{10,... | collective-permute-start | bytes 98312 | tf_op jit(solution)/shard_map/ppermute | solution.py:391
  99.8 4.0 %images.16.refs_4_ = f32[32,3584]{1,0:T(8,128)S(1)} custom-call(bf16[3584,4096]{1,0:T(8,128)(2,1)S(1)} %bitcast.15, bf16[32,512]{1,0:T(8,128)(2,1)S(1)} %collective-permute-done.25.refs_0_, bf16[32,512]{1,0:T(8,128)(2,1)S(1)} %collective-permute-done.26.refs_1_, bf16[32,512]{1,0:T(8,128)(2,1)S(1)} %collective-permute-done.27.refs_2_, ...), custom_call_target="tpu_custom_call" | custom-call | flops 4227858432 | bytes 1000000 | tf_op jit(solution)/shard_map/images/pallas_call | solution.py:31
  103.9 5.4 %images.17 = (bf16[32,3584]{1,0:T(8,128)(2,1)S(1)}, bf16[32,128]{1,0:T(8,128)(2,1)S(1)}) custom-call(bf16[3584,4096]{1,0:T(8,128)(2,1)S(1)} %bitcast.16, bf16[32,512]{1,0:T(8,128)(2,1)S(1)} %collective-permute-done.21.refs_0_, bf16[32,512]{1,0:T(8,128)(2,1)S(1)} %collective-permute-done.22.refs_1_, bf16[32,512]{1,0:T(8,128)(2,1)S(1)} %collective-permute-done.23.refs_2_, ...), custom_call_target="tpu_custom_call" | custom-call | flops 5637144576 | bytes 1000000 | tf_op jit(solution)/shard_map/images/pallas_call | solution.py:31
  109.3 2.6 %backs.12 = (bf16[32,640]{1,0:T(8,128)(2,1)S(1)}, bf16[32,640]{1,0:T(8,128)(2,1)S(1)}, bf16[32,640]{1,0:T(8,128)(2,1)S(1)}, bf16[32,640]{1,0:T(8,128)(2,1)S(1)}) custom-call(bf16[3584,4096]{1,0:T(8,128)(2,1)S(1)} %bitcast.17, bf16[32,3584]{1,0:T(8,128)(2,1)S(1)} %get-tuple-element.83.images_ref, bf16[32,128]{1,0:T(8,128)(2,1)S(1)} %get-tuple-element.84.gram_ref), custom_call_target="tpu_custom_call" | custom-call | flops 3758096384 | bytes 1000000 | tf_op jit(solution)/shard_map/backs/pallas_call | solution.py:31
  113.3 1.9 collective-permute-start.33
  115.2 2.6 %backs.13 = (bf16[32,640]{1,0:T(8,128)(2,1)S(1)}, bf16[32,640]{1,0:T(8,128)(2,1)S(1)}, bf16[32,640]{1,0:T(8,128)(2,1)S(1)}, bf16[32,640]{1,0:T(8,128)(2,1)S(1)}) custom-call(bf16[3584,4096]{1,0:T(8,128)(2,1)S(1)} %bitcast.18, bf16[32,3584]{1,0:T(8,128)(2,1)S(1)} %get-tuple-element.83.images_ref, bf16[32,128]{1,0:T(8,128)(2,1)S(1)} %get-tuple-element.84.gram_ref, ...), custom_call_target="tpu_custom_call" | custom-call | flops 3758096384 | bytes 1000000 | tf_op jit(solution)/shard_map/backs/pallas_call | solution.py:31
  117.8 2.2 collective-permute-start.34
  121.2 2.3 collective-permute-start.30
  126.1 2.6 %collective-permute-done.31.refs_4_ = bf16[32,640]{1,0:T(8,128)(2,1)S(1)} collective-permute-done((bf16[32,640]{1,0:T(8,128)(2,1)S(1)}, bf16[32,640]{1,0:T(8,128)(2,1)S(1)}, u32[]{:S(2)}, u32[]{:S(2)}) %collective-permute-start.31) | collective-permute-done | bytes 40992 | tf_op jit(solution)/shard_map/ppermute | solution.py:391
  130.4 1.9 collective-permute-start.40
  133.2 2.4 collective-permute-start.38
  135.7 1.9 collective-permute-start.37
  139.6 3.3 %collective-permute-start.35 = (bf16[32,512]{1,0:T(8,128)(2,1)S(1)}, bf16[32,512]{1,0:T(8,128)(2,1)S(1)}, u32[]{:S(2)}, u32[]{:S(2)}) collective-permute-start(bf16[32,512]{1,0:T(8,128)(2,1)S(1)} %settle.6.refs_0_), channel_id=1, source_target_pairs={{0,4},{1,5},{2,6},{3,7},{4,0},{5,1},{6,2},{7,3},{8,12},{9,13},{10,... | collective-permute-start | bytes 98312 | tf_op jit(solution)/shard_map/ppermute | solution.py:391
  142.8 4.0 %images.19.refs_4_ = f32[32,3584]{1,0:T(8,128)S(1)} custom-call(bf16[3584,4096]{1,0:T(8,128)(2,1)S(1)} %bitcast.21, bf16[32,512]{1,0:T(8,128)(2,1)S(1)} %collective-permute-done.39.refs_0_, bf16[32,512]{1,0:T(8,128)(2,1)S(1)} %collective-permute-done.40.refs_1_, bf16[32,512]{1,0:T(8,128)(2,1)S(1)} %collective-permute-done.41.refs_2_, ...), custom_call_target="tpu_custom_call" | custom-call | flops 4227858432 | bytes 1000000 | tf_op jit(solution)/shard_map/images/pallas_call | solution.py:31
  146.9 5.4 %images.20 = (bf16[32,3584]{1,0:T(8,128)(2,1)S(1)}, bf16[32,128]{1,0:T(8,128)(2,1)S(1)}) custom-call(bf16[3584,4096]{1,0:T(8,128)(2,1)S(1)} %bitcast.22, bf16[32,512]{1,0:T(8,128)(2,1)S(1)} %collective-permute-done.35.refs_0_, bf16[32,512]{1,0:T(8,128)(2,1)S(1)} %collective-permute-done.36.refs_1_, bf16[32,512]{1,0:T(8,128)(2,1)S(1)} %collective-permute-done.37.refs_2_, ...), custom_call_target="tpu_custom_call" | custom-call | flops 5637144576 | bytes 1000000 | tf_op jit(solution)/shard_map/images/pallas_call | solution.py:31
  152.3 2.6 %backs.14 = (bf16[32,640]{1,0:T(8,128)(2,1)S(1)}, bf16[32,640]{1,0:T(8,128)(2,1)S(1)}, bf16[32,640]{1,0:T(8,128)(2,1)S(1)}, bf16[32,640]{1,0:T(8,128)(2,1)S(1)}) custom-call(bf16[3584,4096]{1,0:T(8,128)(2,1)S(1)} %bitcast.23, bf16[32,3584]{1,0:T(8,128)(2,1)S(1)} %get-tuple-element.93.images_ref, bf16[32,128]{1,0:T(8,128)(2,1)S(1)} %get-tuple-element.94.gram_ref), custom_call_target="tpu_custom_call" | custom-call | flops 3758096384 | bytes 1000000 | tf_op jit(solution)/shard_map/backs/pallas_call | solution.py:31
  156.2 1.9 collective-permute-start.47
  158.1 2.6 %backs.15 = (bf16[32,640]{1,0:T(8,128)(2,1)S(1)}, bf16[32,640]{1,0:T(8,128)(2,1)S(1)}, bf16[32,640]{1,0:T(8,128)(2,1)S(1)}, bf16[32,640]{1,0:T(8,128)(2,1)S(1)}) custom-call(bf16[3584,4096]{1,0:T(8,128)(2,1)S(1)} %bitcast.24, bf16[32,3584]{1,0:T(8,128)(2,1)S(1)} %get-tuple-element.93.images_ref, bf16[32,128]{1,0:T(8,128)(2,1)S(1)} %get-tuple-element.94.gram_ref, ...), custom_call_target="tpu_custom_call" | custom-call | flops 3758096384 | bytes 1000000 | tf_op jit(solution)/shard_map/backs/pallas_call | solution.py:31
  160.7 2.3 collective-permute-start.48
  164.1 2.4 collective-permute-start.44
  169.0 2.4 collective-permute-done.45.refs_4_
  172.9 2.0 collective-permute-start.54
  175.9 2.4 collective-permute-start.52
  178.3 1.9 collective-permute-start.51
  180.3 3.3 %collective-permute-start.49 = (bf16[32,512]{1,0:T(8,128)(2,1)S(1)}, bf16[32,512]{1,0:T(8,128)(2,1)S(1)}, u32[]{:S(2)}, u32[]{:S(2)}) collective-permute-start(bf16[32,512]{1,0:T(8,128)(2,1)S(1)} %settle.7.refs_0_), channel_id=1, source_target_pairs={{0,4},{1,5},{2,6},{3,7},{4,0},{5,1},{6,2},{7,3},{8,12},{9,13},{10,... | collective-permute-start | bytes 98312 | tf_op jit(solution)/shard_map/ppermute | solution.py:391
  183.6 2.0 images.21.refs_3_
  187.6 4.0 %images.22.refs_4_ = f32[32,3584]{1,0:T(8,128)S(1)} custom-call(bf16[3584,4096]{1,0:T(8,128)(2,1)S(1)} %bitcast.28, bf16[32,512]{1,0:T(8,128)(2,1)S(1)} %collective-permute-done.53.refs_0_.refs_1_, bf16[32,512]{1,0:T(8,128)(2,1)S(1)} %collective-permute-done.54.refs_1_.refs_2_, bf16[32,512]{1,0:T(8,128)(2,1)S(1)} %collective-permute-done.55.refs_2_.refs_3_, ...), custom_call_target="tpu_custom_call" | custom-call | flops 4227858432 | bytes 1000000 | tf_op jit(solution)/shard_map/images/pallas_call | solution.py:31
  192.4 5.2 %images.23 = (bf16[32,896]{1,0:T(8,128)(2,1)S(1)}, bf16[32,896]{1,0:T(8,128)(2,1)S(1)}, bf16[32,896]{1,0:T(8,128)(2,1)S(1)}, bf16[32,896]{1,0:T(8,128)(2,1)S(1)}) custom-call(bf16[3584,4096]{1,0:T(8,128)(2,1)S(1)} %bitcast.29, bf16[32,512]{1,0:T(8,128)(2,1)S(1)} %collective-permute-done.49.refs_0_.refs_4_, ...), custom_call_target="tpu_custom_call" | custom-call | flops 5637144576 | bytes 1000000 | tf_op jit(solution)/shard_map/images/pallas_call | solution.py:31
  199.7 2.7 %collective-permute-done.57.refs_2_ = bf16[32,896]{1,0:T(8,128)(2,1)S(1)} collective-permute-done((bf16[32,896]{1,0:T(8,128)(2,1)S(1)}, bf16[32,896]{1,0:T(8,128)(2,1)S(1)}, u32[]{:S(2)}, u32[]{:S(2)}) %collective-permute-start.57) | collective-permute-done | bytes 57376 | tf_op jit(solution)/shard_map/ppermute | solution.py:391
  205.1 2.1 collective-permute-start.60
  207.9 2.4 collective-permute-start.62
  211.7 2.0 collective-permute-start.64
  213.7 2.4 collective-permute-start.65
  216.1 2.8 %right_first.1 = (bf16[128,4096]{1,0:T(8,128)(2,1)S(1)}, f32[128,128]{1,0:T(8,128)S(1)}, f32[128,128]{1,0:T(8,128)S(1)}) custom-call(bf16[32,4096]{1,0:T(8,128)(2,1)S(1)} %pack.1.refs_0_, bf16[32,4096]{1,0:T(8,128)(2,1)S(1)} %collective-permute-done.66.refs_1_, bf16[32,4096]{1,0:T(8,128)(2,1)S(1)} %collective-permute-done.67.refs_2_, ...), custom_call_target="tpu_custom_call" | custom-call | flops 100000000 | bytes 1000000 | tf_op jit(solution)/shard_map/right_first/pallas_call | solution.py:31
  222.0 2.9 %right_second.1 = (f32[128,128]{1,0:T(8,128)S(1)}, f32[128,128]{1,0:T(8,128)S(1)}) custom-call(f32[128,128]{1,0:T(8,128)S(1)} %get-tuple-element.116.gram_ref), custom_call_target="tpu_custom_call" | custom-call | flops 100000000 | bytes 1000000 | tf_op jit(solution)/shard_map/right_second/pallas_call | solution.py:31
  224.9 2.5 collective-permute-start.78
  227.4 1.9 collective-permute-start.77
  229.3 3.3 %collective-permute-start.75 = (f32[16,128]{1,0:T(8,128)S(1)}, f32[16,128]{1,0:T(8,128)S(1)}, u32[]{:S(2)}, u32[]{:S(2)}) collective-permute-start(f32[16,128]{1,0:T(8,128)S(1)} %total.3.refs_0_), channel_id=1, source_target_pairs={{0,4},{1,5},{2,6},{3,7},{4,0},{5,1},{6,2},{7,3},{8,12},{9,13},{10,... | collective-permute-start | bytes 24584 | tf_op jit(solution)/shard_map/ppermute | solution.py:391
  232.7 2.5 collective-permute-start.73
  236.1 3.2 %right_third.1.refs_11_ = f32[128,128]{1,0:T(8,128)S(1)} custom-call(f32[128,128]{1,0:T(8,128)S(1)} %get-tuple-element.116.gram_ref, f32[128,128]{1,0:T(8,128)S(1)} %get-tuple-element.117.refs_4_.upper_ref, f32[128,128]{1,0:T(8,128)S(1)} %get-tuple-element.120.lower_ref, f32[128,128]{1,0:T(8,128)S(1)} %get-tuple-element.115.refs_8_.change_ref.refs_10_), custom_call_target="tpu_custom_call" | custom-call | flops 100000000 | bytes 1000000 | tf_op jit(solution)/shard_map/right_third/pallas_call | solution.py:31
  239.4 12.6 %finish.1 = bf16[896,4096]{1,0:T(8,128)(2,1)} custom-call(f32[16,128]{1,0:T(8,128)S(1)} %total.3.refs_0_, f32[16,128]{1,0:T(8,128)S(1)} %collective-permute-done.72.refs_1_, f32[16,128]{1,0:T(8,128)S(1)} %collective-permute-done.73.refs_2_, f32[16,128]{1,0:T(8,128)S(1)} %collective-permute-done.74.refs_3_, f32[16,128]{1,0:T(8,128)S(1)} %collective-permute-done.75.refs_4_, ...), custom_call_target="tpu_custom_call" | custom-call | tf_op jit(solution)/shard_map/finish/pallas_call | solution.py:372
  (131 shorter events, 52.9 us)
Async XLA Ops:
  22.8 12.9 %collective-permute-start.4 = (bf16[32,640]{1,0:T(8,128)(2,1)S(1)}, bf16[32,640]{1,0:T(8,128)(2,1)S(1)}, u32[]{:S(2)}, u32[]{:S(2)}) collective-permute-start(bf16[32,640]{1,0:T(8,128)(2,1)S(1)} %get-tuple-element.70), channel_id=1, source_target_pairs={{0,5},{1,4},{2,7},{3,6},{4,1},{5,0},{6,3},{7,2},{8,13},{9,12},{10,... | collective-permute-start | bytes 122888 | tf_op jit(solution)/shard_map/ppermute | solution.py:391
  27.8 9.9 %collective-permute-start.5 = (bf16[32,640]{1,0:T(8,128)(2,1)S(1)}, bf16[32,640]{1,0:T(8,128)(2,1)S(1)}, u32[]{:S(2)}, u32[]{:S(2)}) collective-permute-start(bf16[32,640]{1,0:T(8,128)(2,1)S(1)} %get-tuple-element.71), channel_id=1, source_target_pairs={{0,6},{1,7},{2,4},{3,5},{4,2},{5,3},{6,0},{7,1},{8,14},{9,15},{10,... | collective-permute-start | bytes 122888 | tf_op jit(solution)/shard_map/ppermute | solution.py:391
  29.1 8.5 %collective-permute-start.6 = (bf16[32,640]{1,0:T(8,128)(2,1)S(1)}, bf16[32,640]{1,0:T(8,128)(2,1)S(1)}, u32[]{:S(2)}, u32[]{:S(2)}) collective-permute-start(bf16[32,640]{1,0:T(8,128)(2,1)S(1)} %get-tuple-element.72), channel_id=1, source_target_pairs={{0,7},{1,6},{2,5},{3,4},{4,3},{5,2},{6,1},{7,0},{8,15},{9,14},{10,... | collective-permute-start | bytes 122888 | tf_op jit(solution)/shard_map/ppermute | solution.py:391
  35.7 5.3 %collective-permute-start.2 = (bf16[32,640]{1,0:T(8,128)(2,1)S(1)}, bf16[32,640]{1,0:T(8,128)(2,1)S(1)}, u32[]{:S(2)}, u32[]{:S(2)}) collective-permute-start(bf16[32,640]{1,0:T(8,128)(2,1)S(1)} %get-tuple-element.69), channel_id=1, source_target_pairs={{0,3},{1,2},{2,1},{3,0},{4,7},{5,6},{6,5},{7,4},{8,11},{9,10},{10,... | collective-permute-start | bytes 122888 | tf_op jit(solution)/shard_map/ppermute | solution.py:391
  37.6 4.9 %collective-permute-start.3 = (bf16[32,640]{1,0:T(8,128)(2,1)S(1)}, bf16[32,640]{1,0:T(8,128)(2,1)S(1)}, u32[]{:S(2)}, u32[]{:S(2)}) collective-permute-start(bf16[32,640]{1,0:T(8,128)(2,1)S(1)} %get-tuple-element.65.out_refs_0_), channel_id=1, source_target_pairs={{0,4},{1,5},{2,6},{3,7},{4,0},{5,1},{6,2},{7,3},{8,12},{9,13},{10,... | collective-permute-start | bytes 122888 | tf_op jit(solution)/shard_map/ppermute | solution.py:391
  43.5 10.2 %collective-permute-start.13 = (bf16[32,512]{1,0:T(8,128)(2,1)S(1)}, bf16[32,512]{1,0:T(8,128)(2,1)S(1)}, u32[]{:S(2)}, u32[]{:S(2)}) collective-permute-start(bf16[32,512]{1,0:T(8,128)(2,1)S(1)} %settle.4.refs_0_), channel_id=1, source_target_pairs={{0,3},{1,2},{2,1},{3,0},{4,7},{5,6},{6,5},{7,4},{8,11},{9,10},{10,... | collective-permute-start | bytes 98312 | tf_op jit(solution)/shard_map/ppermute | solution.py:391
  44.5 9.3 %collective-permute-start.12 = (bf16[32,512]{1,0:T(8,128)(2,1)S(1)}, bf16[32,512]{1,0:T(8,128)(2,1)S(1)}, u32[]{:S(2)}, u32[]{:S(2)}) collective-permute-start(bf16[32,512]{1,0:T(8,128)(2,1)S(1)} %settle.4.refs_0_), channel_id=1, source_target_pairs={{0,2},{1,3},{2,0},{3,1},{4,6},{5,7},{6,4},{7,5},{8,10},{9,11},{10,... | collective-permute-start | bytes 98312 | tf_op jit(solution)/shard_map/ppermute | solution.py:391
  46.5 10.1 %collective-permute-start.11 = (bf16[32,512]{1,0:T(8,128)(2,1)S(1)}, bf16[32,512]{1,0:T(8,128)(2,1)S(1)}, u32[]{:S(2)}, u32[]{:S(2)}) collective-permute-start(bf16[32,512]{1,0:T(8,128)(2,1)S(1)} %settle.4.refs_0_), channel_id=1, source_target_pairs={{0,1},{1,0},{2,3},{3,2},{4,5},{5,4},{6,7},{7,6},{8,9},{9,8},{10,11... | collective-permute-start | bytes 98312 | tf_op jit(solution)/shard_map/ppermute | solution.py:391
  47.0 13.6 %collective-permute-start.10 = (bf16[32,512]{1,0:T(8,128)(2,1)S(1)}, bf16[32,512]{1,0:T(8,128)(2,1)S(1)}, u32[]{:S(2)}, u32[]{:S(2)}) collective-permute-start(bf16[32,512]{1,0:T(8,128)(2,1)S(1)} %settle.4.refs_0_), channel_id=1, source_target_pairs={{0,7},{1,6},{2,5},{3,4},{4,3},{5,2},{6,1},{7,0},{8,15},{9,14},{10,... | collective-permute-start | bytes 98312 | tf_op jit(solution)/shard_map/ppermute | solution.py:391
  49.8 10.9 %collective-permute-start.9 = (bf16[32,512]{1,0:T(8,128)(2,1)S(1)}, bf16[32,512]{1,0:T(8,128)(2,1)S(1)}, u32[]{:S(2)}, u32[]{:S(2)}) collective-permute-start(bf16[32,512]{1,0:T(8,128)(2,1)S(1)} %settle.4.refs_0_), channel_id=1, source_target_pairs={{0,6},{1,7},{2,4},{3,5},{4,2},{5,3},{6,0},{7,1},{8,14},{9,15},{10,... | collective-permute-start | bytes 98312 | tf_op jit(solution)/shard_map/ppermute | solution.py:391
  53.7 7.0 %collective-permute-start.8 = (bf16[32,512]{1,0:T(8,128)(2,1)S(1)}, bf16[32,512]{1,0:T(8,128)(2,1)S(1)}, u32[]{:S(2)}, u32[]{:S(2)}) collective-permute-start(bf16[32,512]{1,0:T(8,128)(2,1)S(1)} %settle.4.refs_0_), channel_id=1, source_target_pairs={{0,5},{1,4},{2,7},{3,6},{4,1},{5,0},{6,3},{7,2},{8,13},{9,12},{10,... | collective-permute-start | bytes 98312 | tf_op jit(solution)/shard_map/ppermute | solution.py:391
  53.8 6.9 %collective-permute-start.7 = (bf16[32,512]{1,0:T(8,128)(2,1)S(1)}, bf16[32,512]{1,0:T(8,128)(2,1)S(1)}, u32[]{:S(2)}, u32[]{:S(2)}) collective-permute-start(bf16[32,512]{1,0:T(8,128)(2,1)S(1)} %settle.4.refs_0_), channel_id=1, source_target_pairs={{0,4},{1,5},{2,6},{3,7},{4,0},{5,1},{6,2},{7,3},{8,12},{9,13},{10,... | collective-permute-start | bytes 98312 | tf_op jit(solution)/shard_map/ppermute | solution.py:391
  68.7 9.6 %collective-permute-start.18 = (bf16[32,640]{1,0:T(8,128)(2,1)S(1)}, bf16[32,640]{1,0:T(8,128)(2,1)S(1)}, u32[]{:S(2)}, u32[]{:S(2)}) collective-permute-start(bf16[32,640]{1,0:T(8,128)(2,1)S(1)} %get-tuple-element.80), channel_id=1, source_target_pairs={{0,5},{1,4},{2,7},{3,6},{4,1},{5,0},{6,3},{7,2},{8,13},{9,12},{10,... | collective-permute-start | bytes 122888 | tf_op jit(solution)/shard_map/ppermute | solution.py:391
  70.4 9.9 %collective-permute-start.19 = (bf16[32,640]{1,0:T(8,128)(2,1)S(1)}, bf16[32,640]{1,0:T(8,128)(2,1)S(1)}, u32[]{:S(2)}, u32[]{:S(2)}) collective-permute-start(bf16[32,640]{1,0:T(8,128)(2,1)S(1)} %get-tuple-element.81), channel_id=1, source_target_pairs={{0,6},{1,7},{2,4},{3,5},{4,2},{5,3},{6,0},{7,1},{8,14},{9,15},{10,... | collective-permute-start | bytes 122888 | tf_op jit(solution)/shard_map/ppermute | solution.py:391
  74.8 6.7 %collective-permute-start.20 = (bf16[32,640]{1,0:T(8,128)(2,1)S(1)}, bf16[32,640]{1,0:T(8,128)(2,1)S(1)}, u32[]{:S(2)}, u32[]{:S(2)}) collective-permute-start(bf16[32,640]{1,0:T(8,128)(2,1)S(1)} %get-tuple-element.82), channel_id=1, source_target_pairs={{0,7},{1,6},{2,5},{3,4},{4,3},{5,2},{6,1},{7,0},{8,15},{9,14},{10,... | collective-permute-start | bytes 122888 | tf_op jit(solution)/shard_map/ppermute | solution.py:391
  78.3 5.1 %collective-permute-start.16 = (bf16[32,640]{1,0:T(8,128)(2,1)S(1)}, bf16[32,640]{1,0:T(8,128)(2,1)S(1)}, u32[]{:S(2)}, u32[]{:S(2)}) collective-permute-start(bf16[32,640]{1,0:T(8,128)(2,1)S(1)} %get-tuple-element.79), channel_id=1, source_target_pairs={{0,3},{1,2},{2,1},{3,0},{4,7},{5,6},{6,5},{7,4},{8,11},{9,10},{10,... | collective-permute-start | bytes 122888 | tf_op jit(solution)/shard_map/ppermute | solution.py:391
  80.3 5.4 %collective-permute-start.17 = (bf16[32,640]{1,0:T(8,128)(2,1)S(1)}, bf16[32,640]{1,0:T(8,128)(2,1)S(1)}, u32[]{:S(2)}, u32[]{:S(2)}) collective-permute-start(bf16[32,640]{1,0:T(8,128)(2,1)S(1)} %get-tuple-element.75.out_refs_0_), channel_id=1, source_target_pairs={{0,4},{1,5},{2,6},{3,7},{4,0},{5,1},{6,2},{7,3},{8,12},{9,13},{10,... | collective-permute-start | bytes 122888 | tf_op jit(solution)/shard_map/ppermute | solution.py:391
  86.7 9.9 %collective-permute-start.27 = (bf16[32,512]{1,0:T(8,128)(2,1)S(1)}, bf16[32,512]{1,0:T(8,128)(2,1)S(1)}, u32[]{:S(2)}, u32[]{:S(2)}) collective-permute-start(bf16[32,512]{1,0:T(8,128)(2,1)S(1)} %settle.5.refs_0_), channel_id=1, source_target_pairs={{0,3},{1,2},{2,1},{3,0},{4,7},{5,6},{6,5},{7,4},{8,11},{9,10},{10,... | collective-permute-start | bytes 98312 | tf_op jit(solution)/shard_map/ppermute | solution.py:391
  87.2 9.5 %collective-permute-start.26 = (bf16[32,512]{1,0:T(8,128)(2,1)S(1)}, bf16[32,512]{1,0:T(8,128)(2,1)S(1)}, u32[]{:S(2)}, u32[]{:S(2)}) collective-permute-start(bf16[32,512]{1,0:T(8,128)(2,1)S(1)} %settle.5.refs_0_), channel_id=1, source_target_pairs={{0,2},{1,3},{2,0},{3,1},{4,6},{5,7},{6,4},{7,5},{8,10},{9,11},{10,... | collective-permute-start | bytes 98312 | tf_op jit(solution)/shard_map/ppermute | solution.py:391
  89.4 10.4 %collective-permute-start.25 = (bf16[32,512]{1,0:T(8,128)(2,1)S(1)}, bf16[32,512]{1,0:T(8,128)(2,1)S(1)}, u32[]{:S(2)}, u32[]{:S(2)}) collective-permute-start(bf16[32,512]{1,0:T(8,128)(2,1)S(1)} %settle.5.refs_0_), channel_id=1, source_target_pairs={{0,1},{1,0},{2,3},{3,2},{4,5},{5,4},{6,7},{7,6},{8,9},{9,8},{10,11... | collective-permute-start | bytes 98312 | tf_op jit(solution)/shard_map/ppermute | solution.py:391
  90.2 13.7 %collective-permute-start.24 = (bf16[32,512]{1,0:T(8,128)(2,1)S(1)}, bf16[32,512]{1,0:T(8,128)(2,1)S(1)}, u32[]{:S(2)}, u32[]{:S(2)}) collective-permute-start(bf16[32,512]{1,0:T(8,128)(2,1)S(1)} %settle.5.refs_0_), channel_id=1, source_target_pairs={{0,7},{1,6},{2,5},{3,4},{4,3},{5,2},{6,1},{7,0},{8,15},{9,14},{10,... | collective-permute-start | bytes 98312 | tf_op jit(solution)/shard_map/ppermute | solution.py:391
  92.8 11.1 %collective-permute-start.23 = (bf16[32,512]{1,0:T(8,128)(2,1)S(1)}, bf16[32,512]{1,0:T(8,128)(2,1)S(1)}, u32[]{:S(2)}, u32[]{:S(2)}) collective-permute-start(bf16[32,512]{1,0:T(8,128)(2,1)S(1)} %settle.5.refs_0_), channel_id=1, source_target_pairs={{0,6},{1,7},{2,4},{3,5},{4,2},{5,3},{6,0},{7,1},{8,14},{9,15},{10,... | collective-permute-start | bytes 98312 | tf_op jit(solution)/shard_map/ppermute | solution.py:391
  96.6 7.3 %collective-permute-start.22 = (bf16[32,512]{1,0:T(8,128)(2,1)S(1)}, bf16[32,512]{1,0:T(8,128)(2,1)S(1)}, u32[]{:S(2)}, u32[]{:S(2)}) collective-permute-start(bf16[32,512]{1,0:T(8,128)(2,1)S(1)} %settle.5.refs_0_), channel_id=1, source_target_pairs={{0,5},{1,4},{2,7},{3,6},{4,1},{5,0},{6,3},{7,2},{8,13},{9,12},{10,... | collective-permute-start | bytes 98312 | tf_op jit(solution)/shard_map/ppermute | solution.py:391
  96.7 7.2 %collective-permute-start.21 = (bf16[32,512]{1,0:T(8,128)(2,1)S(1)}, bf16[32,512]{1,0:T(8,128)(2,1)S(1)}, u32[]{:S(2)}, u32[]{:S(2)}) collective-permute-start(bf16[32,512]{1,0:T(8,128)(2,1)S(1)} %settle.5.refs_0_), channel_id=1, source_target_pairs={{0,4},{1,5},{2,6},{3,7},{4,0},{5,1},{6,2},{7,3},{8,12},{9,13},{10,... | collective-permute-start | bytes 98312 | tf_op jit(solution)/shard_map/ppermute | solution.py:391
  111.9 9.3 %collective-permute-start.32 = (bf16[32,640]{1,0:T(8,128)(2,1)S(1)}, bf16[32,640]{1,0:T(8,128)(2,1)S(1)}, u32[]{:S(2)}, u32[]{:S(2)}) collective-permute-start(bf16[32,640]{1,0:T(8,128)(2,1)S(1)} %get-tuple-element.90), channel_id=1, source_target_pairs={{0,5},{1,4},{2,7},{3,6},{4,1},{5,0},{6,3},{7,2},{8,13},{9,12},{10,... | collective-permute-start | bytes 122888 | tf_op jit(solution)/shard_map/ppermute | solution.py:391
  113.3 10.2 %collective-permute-start.33 = (bf16[32,640]{1,0:T(8,128)(2,1)S(1)}, bf16[32,640]{1,0:T(8,128)(2,1)S(1)}, u32[]{:S(2)}, u32[]{:S(2)}) collective-permute-start(bf16[32,640]{1,0:T(8,128)(2,1)S(1)} %get-tuple-element.91), channel_id=1, source_target_pairs={{0,6},{1,7},{2,4},{3,5},{4,2},{5,3},{6,0},{7,1},{8,14},{9,15},{10,... | collective-permute-start | bytes 122888 | tf_op jit(solution)/shard_map/ppermute | solution.py:391
  117.8 6.8 %collective-permute-start.34 = (bf16[32,640]{1,0:T(8,128)(2,1)S(1)}, bf16[32,640]{1,0:T(8,128)(2,1)S(1)}, u32[]{:S(2)}, u32[]{:S(2)}) collective-permute-start(bf16[32,640]{1,0:T(8,128)(2,1)S(1)} %get-tuple-element.92), channel_id=1, source_target_pairs={{0,7},{1,6},{2,5},{3,4},{4,3},{5,2},{6,1},{7,0},{8,15},{9,14},{10,... | collective-permute-start | bytes 122888 | tf_op jit(solution)/shard_map/ppermute | solution.py:391
  121.2 4.9 %collective-permute-start.30 = (bf16[32,640]{1,0:T(8,128)(2,1)S(1)}, bf16[32,640]{1,0:T(8,128)(2,1)S(1)}, u32[]{:S(2)}, u32[]{:S(2)}) collective-permute-start(bf16[32,640]{1,0:T(8,128)(2,1)S(1)} %get-tuple-element.89), channel_id=1, source_target_pairs={{0,3},{1,2},{2,1},{3,0},{4,7},{5,6},{6,5},{7,4},{8,11},{9,10},{10,... | collective-permute-start | bytes 122888 | tf_op jit(solution)/shard_map/ppermute | solution.py:391
  123.5 5.3 %collective-permute-start.31 = (bf16[32,640]{1,0:T(8,128)(2,1)S(1)}, bf16[32,640]{1,0:T(8,128)(2,1)S(1)}, u32[]{:S(2)}, u32[]{:S(2)}) collective-permute-start(bf16[32,640]{1,0:T(8,128)(2,1)S(1)} %get-tuple-element.85.out_refs_0_), channel_id=1, source_target_pairs={{0,4},{1,5},{2,6},{3,7},{4,0},{5,1},{6,2},{7,3},{8,12},{9,13},{10,... | collective-permute-start | bytes 122888 | tf_op jit(solution)/shard_map/ppermute | solution.py:391
  129.7 9.7 %collective-permute-start.41 = (bf16[32,512]{1,0:T(8,128)(2,1)S(1)}, bf16[32,512]{1,0:T(8,128)(2,1)S(1)}, u32[]{:S(2)}, u32[]{:S(2)}) collective-permute-start(bf16[32,512]{1,0:T(8,128)(2,1)S(1)} %settle.6.refs_0_), channel_id=1, source_target_pairs={{0,3},{1,2},{2,1},{3,0},{4,7},{5,6},{6,5},{7,4},{8,11},{9,10},{10,... | collective-permute-start | bytes 98312 | tf_op jit(solution)/shard_map/ppermute | solution.py:391
  130.4 9.1 %collective-permute-start.40 = (bf16[32,512]{1,0:T(8,128)(2,1)S(1)}, bf16[32,512]{1,0:T(8,128)(2,1)S(1)}, u32[]{:S(2)}, u32[]{:S(2)}) collective-permute-start(bf16[32,512]{1,0:T(8,128)(2,1)S(1)} %settle.6.refs_0_), channel_id=1, source_target_pairs={{0,2},{1,3},{2,0},{3,1},{4,6},{5,7},{6,4},{7,5},{8,10},{9,11},{10,... | collective-permute-start | bytes 98312 | tf_op jit(solution)/shard_map/ppermute | solution.py:391
  132.3 10.5 %collective-permute-start.39 = (bf16[32,512]{1,0:T(8,128)(2,1)S(1)}, bf16[32,512]{1,0:T(8,128)(2,1)S(1)}, u32[]{:S(2)}, u32[]{:S(2)}) collective-permute-start(bf16[32,512]{1,0:T(8,128)(2,1)S(1)} %settle.6.refs_0_), channel_id=1, source_target_pairs={{0,1},{1,0},{2,3},{3,2},{4,5},{5,4},{6,7},{7,6},{8,9},{9,8},{10,11... | collective-permute-start | bytes 98312 | tf_op jit(solution)/shard_map/ppermute | solution.py:391
  133.2 13.6 %collective-permute-start.38 = (bf16[32,512]{1,0:T(8,128)(2,1)S(1)}, bf16[32,512]{1,0:T(8,128)(2,1)S(1)}, u32[]{:S(2)}, u32[]{:S(2)}) collective-permute-start(bf16[32,512]{1,0:T(8,128)(2,1)S(1)} %settle.6.refs_0_), channel_id=1, source_target_pairs={{0,7},{1,6},{2,5},{3,4},{4,3},{5,2},{6,1},{7,0},{8,15},{9,14},{10,... | collective-permute-start | bytes 98312 | tf_op jit(solution)/shard_map/ppermute | solution.py:391
  135.7 11.2 %collective-permute-start.37 = (bf16[32,512]{1,0:T(8,128)(2,1)S(1)}, bf16[32,512]{1,0:T(8,128)(2,1)S(1)}, u32[]{:S(2)}, u32[]{:S(2)}) collective-permute-start(bf16[32,512]{1,0:T(8,128)(2,1)S(1)} %settle.6.refs_0_), channel_id=1, source_target_pairs={{0,6},{1,7},{2,4},{3,5},{4,2},{5,3},{6,0},{7,1},{8,14},{9,15},{10,... | collective-permute-start | bytes 98312 | tf_op jit(solution)/shard_map/ppermute | solution.py:391
  139.5 7.4 %collective-permute-start.36 = (bf16[32,512]{1,0:T(8,128)(2,1)S(1)}, bf16[32,512]{1,0:T(8,128)(2,1)S(1)}, u32[]{:S(2)}, u32[]{:S(2)}) collective-permute-start(bf16[32,512]{1,0:T(8,128)(2,1)S(1)} %settle.6.refs_0_), channel_id=1, source_target_pairs={{0,5},{1,4},{2,7},{3,6},{4,1},{5,0},{6,3},{7,2},{8,13},{9,12},{10,... | collective-permute-start | bytes 98312 | tf_op jit(solution)/shard_map/ppermute | solution.py:391
  139.6 7.3 %collective-permute-start.35 = (bf16[32,512]{1,0:T(8,128)(2,1)S(1)}, bf16[32,512]{1,0:T(8,128)(2,1)S(1)}, u32[]{:S(2)}, u32[]{:S(2)}) collective-permute-start(bf16[32,512]{1,0:T(8,128)(2,1)S(1)} %settle.6.refs_0_), channel_id=1, source_target_pairs={{0,4},{1,5},{2,6},{3,7},{4,0},{5,1},{6,2},{7,3},{8,12},{9,13},{10,... | collective-permute-start | bytes 98312 | tf_op jit(solution)/shard_map/ppermute | solution.py:391
  154.9 9.2 %collective-permute-start.46 = (bf16[32,640]{1,0:T(8,128)(2,1)S(1)}, bf16[32,640]{1,0:T(8,128)(2,1)S(1)}, u32[]{:S(2)}, u32[]{:S(2)}) collective-permute-start(bf16[32,640]{1,0:T(8,128)(2,1)S(1)} %get-tuple-element.100), channel_id=1, source_target_pairs={{0,5},{1,4},{2,7},{3,6},{4,1},{5,0},{6,3},{7,2},{8,13},{9,12},{10,... | collective-permute-start | bytes 122888 | tf_op jit(solution)/shard_map/ppermute | solution.py:391
  156.2 10.3 %collective-permute-start.47 = (bf16[32,640]{1,0:T(8,128)(2,1)S(1)}, bf16[32,640]{1,0:T(8,128)(2,1)S(1)}, u32[]{:S(2)}, u32[]{:S(2)}) collective-permute-start(bf16[32,640]{1,0:T(8,128)(2,1)S(1)} %get-tuple-element.101), channel_id=1, source_target_pairs={{0,6},{1,7},{2,4},{3,5},{4,2},{5,3},{6,0},{7,1},{8,14},{9,15},{10,... | collective-permute-start | bytes 122888 | tf_op jit(solution)/shard_map/ppermute | solution.py:391
  160.7 7.1 %collective-permute-start.48 = (bf16[32,640]{1,0:T(8,128)(2,1)S(1)}, bf16[32,640]{1,0:T(8,128)(2,1)S(1)}, u32[]{:S(2)}, u32[]{:S(2)}) collective-permute-start(bf16[32,640]{1,0:T(8,128)(2,1)S(1)} %get-tuple-element.102), channel_id=1, source_target_pairs={{0,7},{1,6},{2,5},{3,4},{4,3},{5,2},{6,1},{7,0},{8,15},{9,14},{10,... | collective-permute-start | bytes 122888 | tf_op jit(solution)/shard_map/ppermute | solution.py:391
  164.1 4.9 %collective-permute-start.44 = (bf16[32,640]{1,0:T(8,128)(2,1)S(1)}, bf16[32,640]{1,0:T(8,128)(2,1)S(1)}, u32[]{:S(2)}, u32[]{:S(2)}) collective-permute-start(bf16[32,640]{1,0:T(8,128)(2,1)S(1)} %get-tuple-element.99), channel_id=1, source_target_pairs={{0,3},{1,2},{2,1},{3,0},{4,7},{5,6},{6,5},{7,4},{8,11},{9,10},{10,... | collective-permute-start | bytes 122888 | tf_op jit(solution)/shard_map/ppermute | solution.py:391
  166.5 4.9 %collective-permute-start.45 = (bf16[32,640]{1,0:T(8,128)(2,1)S(1)}, bf16[32,640]{1,0:T(8,128)(2,1)S(1)}, u32[]{:S(2)}, u32[]{:S(2)}) collective-permute-start(bf16[32,640]{1,0:T(8,128)(2,1)S(1)} %get-tuple-element.95.out_refs_0_), channel_id=1, source_target_pairs={{0,4},{1,5},{2,6},{3,7},{4,0},{5,1},{6,2},{7,3},{8,12},{9,13},{10,... | collective-permute-start | bytes 122888 | tf_op jit(solution)/shard_map/ppermute | solution.py:391
  172.4 7.9 %collective-permute-start.55 = (bf16[32,512]{1,0:T(8,128)(2,1)S(1)}, bf16[32,512]{1,0:T(8,128)(2,1)S(1)}, u32[]{:S(2)}, u32[]{:S(2)}) collective-permute-start(bf16[32,512]{1,0:T(8,128)(2,1)S(1)} %settle.7.refs_0_), channel_id=1, source_target_pairs={{0,3},{1,2},{2,1},{3,0},{4,7},{5,6},{6,5},{7,4},{8,11},{9,10},{10,... | collective-permute-start | bytes 98312 | tf_op jit(solution)/shard_map/ppermute | solution.py:391
  172.9 7.3 %collective-permute-start.54 = (bf16[32,512]{1,0:T(8,128)(2,1)S(1)}, bf16[32,512]{1,0:T(8,128)(2,1)S(1)}, u32[]{:S(2)}, u32[]{:S(2)}) collective-permute-start(bf16[32,512]{1,0:T(8,128)(2,1)S(1)} %settle.7.refs_0_), channel_id=1, source_target_pairs={{0,2},{1,3},{2,0},{3,1},{4,6},{5,7},{6,4},{7,5},{8,10},{9,11},{10,... | collective-permute-start | bytes 98312 | tf_op jit(solution)/shard_map/ppermute | solution.py:391
  175.0 10.6 %collective-permute-start.53 = (bf16[32,512]{1,0:T(8,128)(2,1)S(1)}, bf16[32,512]{1,0:T(8,128)(2,1)S(1)}, u32[]{:S(2)}, u32[]{:S(2)}) collective-permute-start(bf16[32,512]{1,0:T(8,128)(2,1)S(1)} %settle.7.refs_0_), channel_id=1, source_target_pairs={{0,1},{1,0},{2,3},{3,2},{4,5},{5,4},{6,7},{7,6},{8,9},{9,8},{10,11... | collective-permute-start | bytes 98312 | tf_op jit(solution)/shard_map/ppermute | solution.py:391
  175.9 9.7 %collective-permute-start.52 = (bf16[32,512]{1,0:T(8,128)(2,1)S(1)}, bf16[32,512]{1,0:T(8,128)(2,1)S(1)}, u32[]{:S(2)}, u32[]{:S(2)}) collective-permute-start(bf16[32,512]{1,0:T(8,128)(2,1)S(1)} %settle.7.refs_0_), channel_id=1, source_target_pairs={{0,7},{1,6},{2,5},{3,4},{4,3},{5,2},{6,1},{7,0},{8,15},{9,14},{10,... | collective-permute-start | bytes 98312 | tf_op jit(solution)/shard_map/ppermute | solution.py:391
  178.3 7.2 %collective-permute-start.51 = (bf16[32,512]{1,0:T(8,128)(2,1)S(1)}, bf16[32,512]{1,0:T(8,128)(2,1)S(1)}, u32[]{:S(2)}, u32[]{:S(2)}) collective-permute-start(bf16[32,512]{1,0:T(8,128)(2,1)S(1)} %settle.7.refs_0_), channel_id=1, source_target_pairs={{0,6},{1,7},{2,4},{3,5},{4,2},{5,3},{6,0},{7,1},{8,14},{9,15},{10,... | collective-permute-start | bytes 98312 | tf_op jit(solution)/shard_map/ppermute | solution.py:391
  180.3 5.7 %collective-permute-start.50 = (bf16[32,512]{1,0:T(8,128)(2,1)S(1)}, bf16[32,512]{1,0:T(8,128)(2,1)S(1)}, u32[]{:S(2)}, u32[]{:S(2)}) collective-permute-start(bf16[32,512]{1,0:T(8,128)(2,1)S(1)} %settle.7.refs_0_), channel_id=1, source_target_pairs={{0,5},{1,4},{2,7},{3,6},{4,1},{5,0},{6,3},{7,2},{8,13},{9,12},{10,... | collective-permute-start | bytes 98312 | tf_op jit(solution)/shard_map/ppermute | solution.py:391
  180.3 5.7 %collective-permute-start.49 = (bf16[32,512]{1,0:T(8,128)(2,1)S(1)}, bf16[32,512]{1,0:T(8,128)(2,1)S(1)}, u32[]{:S(2)}, u32[]{:S(2)}) collective-permute-start(bf16[32,512]{1,0:T(8,128)(2,1)S(1)} %settle.7.refs_0_), channel_id=1, source_target_pairs={{0,4},{1,5},{2,6},{3,7},{4,0},{5,1},{6,2},{7,3},{8,12},{9,13},{10,... | collective-permute-start | bytes 98312 | tf_op jit(solution)/shard_map/ppermute | solution.py:391
  186.0 6.4 %collective-permute-start.67 = (bf16[32,4096]{1,0:T(8,128)(2,1)S(1)}, bf16[32,4096]{1,0:T(8,128)(2,1)S(1)}, u32[]{:S(2)}, u32[]{:S(2)}) collective-permute-start(bf16[32,4096]{1,0:T(8,128)(2,1)S(1)} %pack.1.refs_0_), channel_id=1, source_target_pairs={{0,16},{8,24},{16,0},{24,8},{1,17},{9,25},{17,1},{25,9},{2,18},{10... | collective-permute-start | bytes 786440 | tf_op jit(solution)/shard_map/ppermute | solution.py:391
  187.6 24.2 %collective-permute-start.66 = (bf16[32,4096]{1,0:T(8,128)(2,1)S(1)}, bf16[32,4096]{1,0:T(8,128)(2,1)S(1)}, u32[]{:S(2)}, u32[]{:S(2)}) collective-permute-start(bf16[32,4096]{1,0:T(8,128)(2,1)S(1)} %pack.1.refs_0_), channel_id=1, source_target_pairs={{0,8},{8,0},{16,24},{24,16},{1,9},{9,1},{17,25},{25,17},{2,10},{10... | collective-permute-start | bytes 786440 | tf_op jit(solution)/shard_map/ppermute | solution.py:391
  192.4 21.2 %collective-permute-start.68 = (bf16[32,4096]{1,0:T(8,128)(2,1)S(1)}, bf16[32,4096]{1,0:T(8,128)(2,1)S(1)}, u32[]{:S(2)}, u32[]{:S(2)}) collective-permute-start(bf16[32,4096]{1,0:T(8,128)(2,1)S(1)} %collective-permute-done.67.refs_2_), channel_id=1, source_target_pairs={{0,8},{8,0},{16,24},{24,16},{1,9},{9,1},{17,25},{25,17},{2,10},{10... | collective-permute-start | bytes 786440 | tf_op jit(solution)/shard_map/ppermute | solution.py:391
  205.1 5.1 %collective-permute-start.60 = (f32[16,128]{1,0:T(8,128)S(1)}, f32[16,128]{1,0:T(8,128)S(1)}, u32[]{:S(2)}, u32[]{:S(2)}) collective-permute-start(f32[16,128]{1,0:T(8,128)S(1)} %get-tuple-element.109), channel_id=1, source_target_pairs={{0,2},{1,3},{2,0},{3,1},{4,6},{5,7},{6,4},{7,5},{8,10},{9,11},{10,... | collective-permute-start | bytes 24584 | tf_op jit(solution)/shard_map/ppermute | solution.py:391
  207.2 11.7 %collective-permute-start.61 = (f32[16,128]{1,0:T(8,128)S(1)}, f32[16,128]{1,0:T(8,128)S(1)}, u32[]{:S(2)}, u32[]{:S(2)}) collective-permute-start(f32[16,128]{1,0:T(8,128)S(1)} %get-tuple-element.110), channel_id=1, source_target_pairs={{0,3},{1,2},{2,1},{3,0},{4,7},{5,6},{6,5},{7,4},{8,11},{9,10},{10,... | collective-permute-start | bytes 24584 | tf_op jit(solution)/shard_map/ppermute | solution.py:391
  207.9 11.1 %collective-permute-start.62 = (f32[16,128]{1,0:T(8,128)S(1)}, f32[16,128]{1,0:T(8,128)S(1)}, u32[]{:S(2)}, u32[]{:S(2)}) collective-permute-start(f32[16,128]{1,0:T(8,128)S(1)} %get-tuple-element.111), channel_id=1, source_target_pairs={{0,4},{1,5},{2,6},{3,7},{4,0},{5,1},{6,2},{7,3},{8,12},{9,13},{10,... | collective-permute-start | bytes 24584 | tf_op jit(solution)/shard_map/ppermute | solution.py:391
  210.3 8.7 %collective-permute-start.63 = (f32[16,128]{1,0:T(8,128)S(1)}, f32[16,128]{1,0:T(8,128)S(1)}, u32[]{:S(2)}, u32[]{:S(2)}) collective-permute-start(f32[16,128]{1,0:T(8,128)S(1)} %get-tuple-element.112), channel_id=1, source_target_pairs={{0,5},{1,4},{2,7},{3,6},{4,1},{5,0},{6,3},{7,2},{8,13},{9,12},{10,... | collective-permute-start | bytes 24584 | tf_op jit(solution)/shard_map/ppermute | solution.py:391
  211.7 7.2 %collective-permute-start.64 = (f32[16,128]{1,0:T(8,128)S(1)}, f32[16,128]{1,0:T(8,128)S(1)}, u32[]{:S(2)}, u32[]{:S(2)}) collective-permute-start(f32[16,128]{1,0:T(8,128)S(1)} %get-tuple-element.113), channel_id=1, source_target_pairs={{0,6},{1,7},{2,4},{3,5},{4,2},{5,3},{6,0},{7,1},{8,14},{9,15},{10,... | collective-permute-start | bytes 24584 | tf_op jit(solution)/shard_map/ppermute | solution.py:391
  213.7 6.3 %collective-permute-start.65 = (f32[16,128]{1,0:T(8,128)S(1)}, f32[16,128]{1,0:T(8,128)S(1)}, u32[]{:S(2)}, u32[]{:S(2)}) collective-permute-start(f32[16,128]{1,0:T(8,128)S(1)} %get-tuple-element.114), channel_id=1, source_target_pairs={{0,7},{1,6},{2,5},{3,4},{4,3},{5,2},{6,1},{7,0},{8,15},{9,14},{10,... | collective-permute-start | bytes 24584 | tf_op jit(solution)/shard_map/ppermute | solution.py:391
  220.0 4.8 %collective-permute-start.71 = (f32[16,128]{1,0:T(8,128)S(1)}, f32[16,128]{1,0:T(8,128)S(1)}, u32[]{:S(2)}, u32[]{:S(2)}) collective-permute-start(f32[16,128]{1,0:T(8,128)S(1)} %total.2.refs_0_), channel_id=1, source_target_pairs={{0,24},{8,16},{16,8},{24,0},{1,25},{9,17},{17,9},{25,1},{2,26},{10... | collective-permute-start | bytes 24584 | tf_op jit(solution)/shard_map/ppermute | solution.py:391
  224.9 7.8 %collective-permute-start.78 = (f32[16,128]{1,0:T(8,128)S(1)}, f32[16,128]{1,0:T(8,128)S(1)}, u32[]{:S(2)}, u32[]{:S(2)}) collective-permute-start(f32[16,128]{1,0:T(8,128)S(1)} %total.3.refs_0_), channel_id=1, source_target_pairs={{0,7},{1,6},{2,5},{3,4},{4,3},{5,2},{6,1},{7,0},{8,15},{9,14},{10,... | collective-permute-start | bytes 24584 | tf_op jit(solution)/shard_map/ppermute | solution.py:391
  227.4 7.8 %collective-permute-start.77 = (f32[16,128]{1,0:T(8,128)S(1)}, f32[16,128]{1,0:T(8,128)S(1)}, u32[]{:S(2)}, u32[]{:S(2)}) collective-permute-start(f32[16,128]{1,0:T(8,128)S(1)} %total.3.refs_0_), channel_id=1, source_target_pairs={{0,6},{1,7},{2,4},{3,5},{4,2},{5,3},{6,0},{7,1},{8,14},{9,15},{10,... | collective-permute-start | bytes 24584 | tf_op jit(solution)/shard_map/ppermute | solution.py:391
  229.3 10.1 %collective-permute-start.76 = (f32[16,128]{1,0:T(8,128)S(1)}, f32[16,128]{1,0:T(8,128)S(1)}, u32[]{:S(2)}, u32[]{:S(2)}) collective-permute-start(f32[16,128]{1,0:T(8,128)S(1)} %total.3.refs_0_), channel_id=1, source_target_pairs={{0,5},{1,4},{2,7},{3,6},{4,1},{5,0},{6,3},{7,2},{8,13},{9,12},{10,... | collective-permute-start | bytes 24584 | tf_op jit(solution)/shard_map/ppermute | solution.py:391
  229.3 10.1 %collective-permute-start.75 = (f32[16,128]{1,0:T(8,128)S(1)}, f32[16,128]{1,0:T(8,128)S(1)}, u32[]{:S(2)}, u32[]{:S(2)}) collective-permute-start(f32[16,128]{1,0:T(8,128)S(1)} %total.3.refs_0_), channel_id=1, source_target_pairs={{0,4},{1,5},{2,6},{3,7},{4,0},{5,1},{6,2},{7,3},{8,12},{9,13},{10,... | collective-permute-start | bytes 24584 | tf_op jit(solution)/shard_map/ppermute | solution.py:391
  232.6 6.7 %collective-permute-start.74 = (f32[16,128]{1,0:T(8,128)S(1)}, f32[16,128]{1,0:T(8,128)S(1)}, u32[]{:S(2)}, u32[]{:S(2)}) collective-permute-start(f32[16,128]{1,0:T(8,128)S(1)} %total.3.refs_0_), channel_id=1, source_target_pairs={{0,3},{1,2},{2,1},{3,0},{4,7},{5,6},{6,5},{7,4},{8,11},{9,10},{10,... | collective-permute-start | bytes 24584 | tf_op jit(solution)/shard_map/ppermute | solution.py:391
  232.7 6.7 %collective-permute-start.73 = (f32[16,128]{1,0:T(8,128)S(1)}, f32[16,128]{1,0:T(8,128)S(1)}, u32[]{:S(2)}, u32[]{:S(2)}) collective-permute-start(f32[16,128]{1,0:T(8,128)S(1)} %total.3.refs_0_), channel_id=1, source_target_pairs={{0,2},{1,3},{2,0},{3,1},{4,6},{5,7},{6,4},{7,5},{8,10},{9,11},{10,... | collective-permute-start | bytes 24584 | tf_op jit(solution)/shard_map/ppermute | solution.py:391
  (17 other events, 72.5 us)
